TPU v7x, 512 devices: a whole 4x8x8 slice. The times are simulated.
512 devices in a mesh: gz: 64 (over x, y, core), gy: 8 (over z).
Axes of the slice: x: 4, y: 8, z: 8, core: 2. Of those that a mesh axis runs over, the one named last changes fastest.
Arguments:
- velocity_u: float32 [2, 1536, 8192], P(None, 'gy', 'gz'), may hold values from -6 to 6
- velocity_v: float32 [2, 1536, 8192], P(None, 'gy', 'gz'), may hold values from -6 to 6
- velocity_w: float32 [2, 1536, 8192], P(None, 'gy', 'gz'), may hold values from -6 to 6
- stiffness: float32 [2, 1536, 8192], P(None, 'gy', 'gz'), may hold values from 10 to 1000
- w_in: float32 [3, 128], replicated, may hold values from -3.5 to 3.5
- b_in: float32 [128], replicated, may hold values from -3 to 3
- w_mid: float32 [128, 128], replicated, may hold values from -0.5 to 0.5
- b_mid: float32 [128], replicated, may hold values from -3 to 3
- w_out: float32 [128], replicated, may hold values from -0.5 to 0.5
- cell_list: int32 [2, 262144], P(None, 'gz'), may hold values from 0 to 255
- height_list: int32 [2, 262144], P(None, 'gz'), may hold values from 1 to 8
- face_list: int32 [2, 262144], P(None, 'gz'), may hold values from 0 to 255
- owner_list: int32 [2, 262144, 1], P(None, 'gz'), may hold values from 0 to 63; in each aligned block of 4096 rows (0 to 4095, 4096 to 8191, ..., all dimensions but the last counted through in order) at most 128 rows name the same one
Outputs:
- new_u: float32 [2, 1536, 8192], P(None, 'gy', 'gz')
Inputs may be any that keep to these rules, and one draw needn't show every extreme that they name: `owner_list`: in each aligned block of 4096 rows of one wall (the rows of one device) no owner is named by more than 128 rows, a bound that some block reaches.
All inputs are finite; a program needn't handle non-finite values.
Results may differ from a plain program's by a relative error of at most 0.000067.
Values sent between devices are 32-bit elements; how exact they have to be, the bound alone decides.
A program may use at most 64 MiB of HBM per device.

v0:
```python
import jax
import jax.numpy as jnp
from jax import lax
from jax.sharding import PartitionSpec as P


def padded(shard, sides, width):
    for axis, dim in sides:
        peers, length = (lax.axis_size(axis), shard.shape[dim])
        up = [(i, (i + 1) % peers) for i in range(peers)]
        down = [(j, i) for i, j in up]
        last = lax.slice_in_dim(shard, length - width, length, axis=dim)
        initial = lax.slice_in_dim(shard, 0, width, axis=dim)
        before = lax.ppermute(last, axis, up)
        after = lax.ppermute(initial, axis, down)
        shard = jnp.concatenate([before, shard, after], axis=dim)
    return shard


def shifted(shard, axis, by):
    peers = lax.axis_size(axis)
    pairs = [(i, i + by) for i in range(peers) if 0 <= i + by < peers]
    return lax.ppermute(shard, axis, pairs)


def stress_net(inputs, w_in, b_in, w_mid, b_mid, w_out):
    highest = lax.Precision.HIGHEST
    hidden = jnp.tanh(jnp.dot(w_in.T, inputs, precision=highest) + b_in[:, None])
    hidden = jnp.tanh(jnp.dot(w_mid.T, hidden, precision=highest) + b_mid[:, None])
    return jnp.dot(w_out, hidden, precision=highest)


def local_sweep(keep_rows, weighted, reverse):

    def sweep_step(carry, items):
        value = items[0] * carry[0] + items[1]
        factor = items[0] * carry[1]
        return ((value, factor), (value, factor))

    start = (jnp.zeros_like(weighted[0]), jnp.ones_like(weighted[0]))
    _, outputs = lax.scan(sweep_step, start, (keep_rows, weighted), reverse=reverse)
    return outputs


def sample_at(velocity_u, velocity_v, velocity_w, plane_idx, level_idx, span_idx):
    return jnp.stack(
        [
            velocity_u[plane_idx, level_idx, span_idx],
            velocity_v[plane_idx, level_idx, span_idx],
            velocity_w[plane_idx, level_idx, span_idx],
        ]
    )


def local(
    velocity_u,
    velocity_v,
    velocity_w,
    stiffness,
    w_in,
    b_in,
    w_mid,
    b_mid,
    w_out,
    cell_list,
    height_list,
    face_list,
    owner_list,
):
    planes, level_cells, span_cells = velocity_u.shape
    face_count = planes * span_cells
    devices_z = lax.axis_size("gz")
    level = lax.axis_index("gy")
    levels = lax.axis_size("gy")
    top_side = level == levels - 1
    wall_side = top_side.astype(jnp.int32)
    cells = lax.dynamic_index_in_dim(cell_list, wall_side, 0, keepdims=False)
    heights = lax.dynamic_index_in_dim(height_list, wall_side, 0, keepdims=False)
    faces_of = lax.dynamic_index_in_dim(face_list, wall_side, 0, keepdims=False)
    owners = lax.dynamic_index_in_dim(owner_list, wall_side, 0, keepdims=False)[:, 0]
    row_count = cells.shape[0]
    capacity = 2 * row_count // devices_z
    onehot = (owners[:, None] == jnp.arange(devices_z, dtype=jnp.int32)[None, :]).astype(jnp.int32)
    slots = jnp.sum((jnp.cumsum(onehot, 0) - onehot) * onehot, axis=1)
    face_float = faces_of.astype(jnp.float32)
    level_idx = jnp.where(top_side, level_cells - 1 - heights, heights)
    sample = sample_at(
        velocity_u, velocity_v, velocity_w, cells // span_cells, level_idx, cells % span_cells
    )
    packed = jnp.zeros((4, devices_z, capacity), jnp.float32).at[3].set(float(face_count))
    packed = packed.at[:, owners, slots].set(jnp.concatenate([sample, face_float[None]], 0))
    piece = lax.all_to_all(packed, "gz", split_axis=1, concat_axis=1, tiled=True)
    stress_piece = stress_net(piece[:3].reshape(3, -1), w_in, b_in, w_mid, b_mid, w_out)
    stress_slots = stress_piece.reshape(1, piece.shape[1], piece.shape[2])
    face_slots = piece[3:4]
    face_index = face_slots.reshape(-1).astype(jnp.int32)
    stress_flat = stress_slots.reshape(-1)
    total = jax.ops.segment_sum(stress_flat, face_index, face_count + 1)[:face_count]
    count = jax.ops.segment_sum(jnp.ones_like(stress_flat), face_index, face_count + 1)[:face_count]
    wall_stress = (total / jnp.maximum(count, 1.0)).reshape(planes, span_cells)
    rim_field = padded(velocity_u, (("gz", 2),), 1)
    lateral = rim_field[:, :, 2:] + rim_field[:, :, :-2] - 2.0 * velocity_u
    source = velocity_u + 0.2 * lateral
    bottom_add = jnp.where(level == 0, wall_stress * (1.0 + stiffness[:, 0, :]), 0.0)
    top_add = jnp.where(top_side, wall_stress * (1.0 + stiffness[:, level_cells - 1, :]), 0.0)
    source = source.at[:, 0, :].add(bottom_add)
    source = source.at[:, level_cells - 1, :].add(top_add)
    gain = 1.0 / (1.0 + stiffness)
    keep = stiffness * gain
    keep_rows = jnp.moveaxis(keep, 1, 0)
    gain_rows = jnp.moveaxis(gain, 1, 0)
    source_rows = jnp.moveaxis(source, 1, 0)
    local_fwd, factor_fwd = local_sweep(keep_rows, gain_rows * source_rows, False)
    fwd_total = (factor_fwd[-1], local_fwd[-1])
    zeros_plane = jnp.zeros_like(local_fwd[0])
    fwd_in = zeros_plane
    for round_idx in range(levels - 1):
        fwd_in = shifted(fwd_total[0] * fwd_in + fwd_total[1], "gy", 1)
    forward_val = local_fwd + factor_fwd * fwd_in[None]
    local_back, factor_back = local_sweep(keep_rows, gain_rows * forward_val, True)
    back_total = (factor_back[0], local_back[0])
    back_in = zeros_plane
    for round_idx in range(levels - 1):
        back_in = shifted(back_total[0] * back_in + back_total[1], "gy", -1)
    result_rows = local_back + factor_back * back_in[None]
    return jnp.moveaxis(result_rows, 0, 1)


def solution(mesh):
    in_specs = (
        P(None, "gy", "gz"),
        P(None, "gy", "gz"),
        P(None, "gy", "gz"),
        P(None, "gy", "gz"),
        P(),
        P(),
        P(),
        P(),
        P(),
        P(None, "gz"),
        P(None, "gz"),
        P(None, "gz"),
        P(None, "gz", None),
    )
    out_specs = P(None, "gy", "gz")
    return jax.shard_map(local, mesh=mesh, in_specs=in_specs, out_specs=out_specs, check_vma=False)
```

profile of v0, /device:TPU:192, one launch (start us, length us, event | category | flops | bytes accessed | tf_op | source)
XLA Modules:
  0.0 419.5 jit_solution(17962021321533545685)
XLA Ops:
  1.2 18.4 %reduce-window.6 = s32[64,32,128]{2,1,0:T(8,128)S(1)} reduce-window(s32[64,32,128]{2,1,0:T(8,128)S(1)} %fusion.8, s32[]{:T(128)} %constant.190.clone.1), window={size=1x1x128 pad=0_0x0_0x127_0}, to_apply=%region_0.1 | reduce-window | flops 33292288 | bytes 2097156 | tf_op jit(solution)/shard_map/reduce-window
  22.2 32.9 %gather_fusion = f32[4096]{0:T(1024)S(1)} fusion(f32[2,192,128]{2,1,0:T(8,128)S(1)} %copy-done.1, s32[4096]{0:T(1024)S(1)} %bitcast.171), kind=kCustom, calls=%fused_computation | custom fusion | bytes 81920 | tf_op jit(solution)/shard_map/gather | solution.py:48
  55.2 32.9 %gather_fusion.1 = f32[4096]{0:T(1024)S(1)} fusion(f32[2,192,128]{2,1,0:T(8,128)S(1)} %copy-done, s32[4096]{0:T(1024)S(1)} %bitcast.172), kind=kCustom, calls=%fused_computation.1 | custom fusion | bytes 81920 | tf_op jit(solution)/shard_map/gather | solution.py:49
  88.1 32.9 %gather_fusion.2 = f32[4096]{0:T(1024)S(1)} fusion(f32[2,192,128]{2,1,0:T(8,128)S(1)} %copy-done.2, s32[4096]{0:T(1024)S(1)} %bitcast.173), kind=kCustom, calls=%fused_computation.2 | custom fusion | bytes 81920 | tf_op jit(solution)/shard_map/gather | solution.py:50
  121.9 4.4 %copy.131 = f32[4,8192]{0,1:T(8,128)} copy(f32[4,8192]{0,1:T(8,128)} %constant.213) | data formatting | bytes 262144
  126.3 14.7 %scatter_fusion = f32[4,8192]{0,1:T(8,128)} fusion(f32[4,8192]{0,1:T(8,128)} %copy.131, s32[4096]{0:T(1024)S(1)} %broadcast_select_fusion.1, f32[4096,4]{1,0:T(8,128)S(1)} %copy.62), kind=kCustom, calls=%fused_computation.5 | custom fusion | bytes 212992
  141.0 3.5 copy.63
  144.5 10.7 %all-to-all-start = ((f32[4,64,128]{2,0,1:T(4,128)}), f32[4,64,128]{2,0,1:T(4,128)S(1)}, u32[]{:S(2)}, u32[]{:S(2)}) async-start(f32[4,64,128]{2,0,1:T(4,128)} %copy.63), calls=%async_computation | async-start | bytes 262144 | tf_op jit(solution)/shard_map/all_to_all | solution.py:92
  155.3 6.9 %collective-permute-start = (f32[2,192,1]{2,1,0:T(8,128)S(1)}, f32[2,192,1]{2,1,0:T(8,128)S(1)}, u32[]{:S(2)}, u32[]{:S(2)}) collective-permute-start(f32[2,192,1]{2,1,0:T(8,128)S(1)} %get-tuple-element.329), channel_id=1, source_target_pairs={{8,0},{16,8},{24,16},{32,24},{40,32},{48,40},{56,48},{64,56},{72,6... | collective-permute-start | bytes 4616 | tf_op jit(solution)/shard_map/ppermute | solution.py:15
  162.2 2.1 collective-permute-start.1
  165.3 7.1 %collective-permute-done.1 = f32[2,192,1]{2,1,0:T(8,128)S(1)} collective-permute-done((f32[2,192,1]{2,1,0:T(8,128)S(1)}, f32[2,192,1]{2,1,0:T(8,128)S(1)}, u32[]{:S(2)}, u32[]{:S(2)}) %collective-permute-start.1) | collective-permute-done | bytes 1568 | tf_op jit(solution)/shard_map/ppermute | solution.py:14
  172.8 6.7 %fusion.4 = f32[8192,128]{1,0:T(8,128)S(1)} fusion(f32[3,128]{1,0:T(4,128)S(1)} %copy-done.6, f32[128]{0:T(128)S(1)} %copy-done.8, f32[4,64,128]{2,0,1:T(4,128)S(1)} %all-to-all-done), kind=kOutput, calls=%fused_computation.24 | convolution fusion | flops 38797312 | bytes 4327424 | tf_op jit(solution)/shard_map/dot_general | solution.py:28
  179.5 3.6 fusion.3
  183.2 3.8 fusion.26
  187.0 57.0 %scatter_custom_fusion = f32[257]{0:T(512)S(1)} fusion(s32[8192]{0:T(1024)S(1)} %convert_bitcast_fusion, f32[8192]{0:T(1024)S(1)} %bitcast.187, f32[]{:T(128)} %constant.191.clone.1), kind=kCustom, calls=%fused_computation.109 | custom fusion | flops 8192 | bytes 1032 | tf_op jit(solution)/shard_map/scatter-add | solution.py:98
  244.0 57.0 %scatter_custom_fusion.1 = f32[257]{0:T(512)S(1)} fusion(s32[8192]{0:T(1024)S(1)} %convert_bitcast_fusion, f32[8192]{0:T(1024)S(1)} %broadcast.365, f32[]{:T(128)} %constant.191.clone.1), kind=kCustom, calls=%fused_computation.107 | custom fusion | flops 8192 | bytes 1032 | tf_op jit(solution)/shard_map/scatter-add | solution.py:99
  301.3 11.6 %while.41 = (s32[]{:T(128)}, f32[2,128]{1,0:T(2,128)S(1)}, f32[2,128]{1,0:T(2,128)S(1)}, f32[192,2,128]{2,1,0:T(2,128)S(1)}, f32[192,2,128]{2,1,0:T(2,128)S(1)},...) while((s32[]{:T(128)}, f32[2,128]{1,0:T(2,128)S(1)}, ...), condition=%wide.region_7.8_spmd.clone, body=%wide.region_6.7_spmd.clone.sunk | while | flops 1283 | bytes 10351 | solution.py:41
  313.0 5.5 %collective-permute-start.2 = (f32[2,128]{1,0:T(2,128)S(1)}, f32[2,128]{1,0:T(2,128)S(1)}, u32[]{:S(2)}, u32[]{:S(2)}) collective-permute-start(f32[2,128]{1,0:T(2,128)S(1)} %bitcast_add_fusion.13), channel_id=1, source_target_pairs={{0,1},{1,2},{2,3},{3,4},{4,5},{5,6},{6,7},{8,9},{9,10},{10,11},{11... | collective-permute-start | bytes 3080 | tf_op jit(solution)/shard_map/ppermute | solution.py:23
  319.8 5.4 %collective-permute-start.3 = (f32[2,128]{1,0:T(2,128)S(1)}, f32[2,128]{1,0:T(2,128)S(1)}, u32[]{:S(2)}, u32[]{:S(2)}) collective-permute-start(f32[2,128]{1,0:T(2,128)S(1)} %bitcast_add_fusion.12), channel_id=1, source_target_pairs={{0,1},{1,2},{2,3},{3,4},{4,5},{5,6},{6,7},{8,9},{9,10},{10,11},{11... | collective-permute-start | bytes 3080 | tf_op jit(solution)/shard_map/ppermute | solution.py:23
  326.4 5.4 %collective-permute-start.4 = (f32[2,128]{1,0:T(2,128)S(1)}, f32[2,128]{1,0:T(2,128)S(1)}, u32[]{:S(2)}, u32[]{:S(2)}) collective-permute-start(f32[2,128]{1,0:T(2,128)S(1)} %bitcast_add_fusion.11), channel_id=1, source_target_pairs={{0,1},{1,2},{2,3},{3,4},{4,5},{5,6},{6,7},{8,9},{9,10},{10,11},{11... | collective-permute-start | bytes 3080 | tf_op jit(solution)/shard_map/ppermute | solution.py:23
  333.1 5.4 %collective-permute-start.5 = (f32[2,128]{1,0:T(2,128)S(1)}, f32[2,128]{1,0:T(2,128)S(1)}, u32[]{:S(2)}, u32[]{:S(2)}) collective-permute-start(f32[2,128]{1,0:T(2,128)S(1)} %bitcast_add_fusion.10), channel_id=1, source_target_pairs={{0,1},{1,2},{2,3},{3,4},{4,5},{5,6},{6,7},{8,9},{9,10},{10,11},{11... | collective-permute-start | bytes 3080 | tf_op jit(solution)/shard_map/ppermute | solution.py:23
  339.8 5.4 %collective-permute-start.6 = (f32[2,128]{1,0:T(2,128)S(1)}, f32[2,128]{1,0:T(2,128)S(1)}, u32[]{:S(2)}, u32[]{:S(2)}) collective-permute-start(f32[2,128]{1,0:T(2,128)S(1)} %bitcast_add_fusion.9), channel_id=1, source_target_pairs={{0,1},{1,2},{2,3},{3,4},{4,5},{5,6},{6,7},{8,9},{9,10},{10,11},{11... | collective-permute-start | bytes 3080 | tf_op jit(solution)/shard_map/ppermute | solution.py:23
  346.4 5.4 %collective-permute-start.7 = (f32[2,128]{1,0:T(2,128)S(1)}, f32[2,128]{1,0:T(2,128)S(1)}, u32[]{:S(2)}, u32[]{:S(2)}) collective-permute-start(f32[2,128]{1,0:T(2,128)S(1)} %bitcast_add_fusion.8), channel_id=1, source_target_pairs={{0,1},{1,2},{2,3},{3,4},{4,5},{5,6},{6,7},{8,9},{9,10},{10,11},{11... | collective-permute-start | bytes 3080 | tf_op jit(solution)/shard_map/ppermute | solution.py:23
  353.1 5.4 %collective-permute-start.8 = (f32[2,128]{1,0:T(2,128)S(1)}, f32[2,128]{1,0:T(2,128)S(1)}, u32[]{:S(2)}, u32[]{:S(2)}) collective-permute-start(f32[2,128]{1,0:T(2,128)S(1)} %bitcast_add_fusion.7), channel_id=1, source_target_pairs={{0,1},{1,2},{2,3},{3,4},{4,5},{5,6},{6,7},{8,9},{9,10},{10,11},{11... | collective-permute-start | bytes 3080 | tf_op jit(solution)/shard_map/ppermute | solution.py:23
  359.9 11.9 %while.42 = (s32[]{:T(128)}, f32[2,128]{1,0:T(2,128)S(1)}, f32[2,128]{1,0:T(2,128)S(1)}, f32[192,2,128]{2,1,0:T(2,128)S(1)}, f32[192,2,128]{2,1,0:T(2,128)S(1)},...) while((s32[]{:T(128)}, f32[2,128]{1,0:T(2,128)S(1)}, ...), condition=%wide.region_9.10_spmd.clone, body=%wide.region_8.9_spmd.clone.sunk | while | flops 1284 | bytes 10371 | solution.py:41
  373.8 5.0 %collective-permute-done.9 = f32[2,128]{1,0:T(2,128)S(1)} collective-permute-done((f32[2,128]{1,0:T(2,128)S(1)}, f32[2,128]{1,0:T(2,128)S(1)}, u32[]{:S(2)}, u32[]{:S(2)}) %collective-permute-start.9) | collective-permute-done | bytes 1056 | tf_op jit(solution)/shard_map/ppermute | solution.py:23
  380.7 4.7 %collective-permute-done.10 = f32[2,128]{1,0:T(2,128)S(1)} collective-permute-done((f32[2,128]{1,0:T(2,128)S(1)}, f32[2,128]{1,0:T(2,128)S(1)}, u32[]{:S(2)}, u32[]{:S(2)}) %collective-permute-start.10) | collective-permute-done | bytes 1056 | tf_op jit(solution)/shard_map/ppermute | solution.py:23
  387.4 4.7 %collective-permute-done.11 = f32[2,128]{1,0:T(2,128)S(1)} collective-permute-done((f32[2,128]{1,0:T(2,128)S(1)}, f32[2,128]{1,0:T(2,128)S(1)}, u32[]{:S(2)}, u32[]{:S(2)}) %collective-permute-start.11) | collective-permute-done | bytes 1056 | tf_op jit(solution)/shard_map/ppermute | solution.py:23
  394.0 4.7 %collective-permute-done.12 = f32[2,128]{1,0:T(2,128)S(1)} collective-permute-done((f32[2,128]{1,0:T(2,128)S(1)}, f32[2,128]{1,0:T(2,128)S(1)}, u32[]{:S(2)}, u32[]{:S(2)}) %collective-permute-start.12) | collective-permute-done | bytes 1056 | tf_op jit(solution)/shard_map/ppermute | solution.py:23
  400.7 4.7 %collective-permute-done.13 = f32[2,128]{1,0:T(2,128)S(1)} collective-permute-done((f32[2,128]{1,0:T(2,128)S(1)}, f32[2,128]{1,0:T(2,128)S(1)}, u32[]{:S(2)}, u32[]{:S(2)}) %collective-permute-start.13) | collective-permute-done | bytes 1056 | tf_op jit(solution)/shard_map/ppermute | solution.py:23
  407.4 4.7 %collective-permute-done.14 = f32[2,128]{1,0:T(2,128)S(1)} collective-permute-done((f32[2,128]{1,0:T(2,128)S(1)}, f32[2,128]{1,0:T(2,128)S(1)}, u32[]{:S(2)}, u32[]{:S(2)}) %collective-permute-start.14) | collective-permute-done | bytes 1056 | tf_op jit(solution)/shard_map/ppermute | solution.py:23
  414.0 4.7 %collective-permute-done.15 = f32[2,128]{1,0:T(2,128)S(1)} collective-permute-done((f32[2,128]{1,0:T(2,128)S(1)}, f32[2,128]{1,0:T(2,128)S(1)}, u32[]{:S(2)}, u32[]{:S(2)}) %collective-permute-start.15) | collective-permute-done | bytes 1056 | tf_op jit(solution)/shard_map/ppermute | solution.py:23
  (859 shorter events, 41.1 us)
Async XLA Ops:
  0.0 55.2 %copy-start = (f32[2,192,128]{2,1,0:T(8,128)S(1)}, f32[2,192,128]{2,1,0:T(8,128)}, u32[]{:S(2)}) copy-start(f32[2,192,128]{2,1,0:T(8,128)} %param.24) | copy-start | bytes 589828
  20.0 1.9 copy-start.11
  20.0 2.1 copy-start.10
  20.0 2.2 copy-start.1
  55.2 33.0 %copy-start.2 = (f32[2,192,128]{2,1,0:T(8,128)S(1)}, f32[2,192,128]{2,1,0:T(8,128)}, u32[]{:S(2)}) copy-start(f32[2,192,128]{2,1,0:T(8,128)} %param.25) | copy-start | bytes 589828
  88.1 33.0 %copy-start.5 = (s32[2,4096]{1,0:T(2,128)S(1)}, s32[2,4096]{1,0:T(2,128)}, u32[]{:S(2)}) copy-start(s32[2,4096]{1,0:T(2,128)} %param.34) | copy-start | bytes 98308
  141.0 23.3 %copy-start.3 = (f32[2,192,128]{2,1,0:T(8,128)S(1)}, f32[2,192,128]{2,1,0:T(8,128)}, u32[]{:S(2)}) copy-start(f32[2,192,128]{2,1,0:T(8,128)} %param.26) | copy-start | bytes 589828
  144.5 28.3 %copy-start.6 = (f32[3,128]{1,0:T(4,128)S(1)}, f32[3,128]{1,0:T(4,128)}, u32[]{:S(2)}) copy-start(f32[3,128]{1,0:T(4,128)} %param.27) | copy-start | bytes 4612
  144.5 28.3 %copy-start.8 = (f32[128]{0:T(128)S(1)}, f32[128]{0:T(128)}, u32[]{:S(2)}) copy-start(f32[128]{0:T(128)} %param.28) | copy-start | bytes 1540
  144.5 28.2 %all-to-all-start = ((f32[4,64,128]{2,0,1:T(4,128)}), f32[4,64,128]{2,0,1:T(4,128)S(1)}, u32[]{:S(2)}, u32[]{:S(2)}) async-start(f32[4,64,128]{2,0,1:T(4,128)} %copy.63), calls=%async_computation | async-start | bytes 262144 | tf_op jit(solution)/shard_map/all_to_all | solution.py:92
  155.3 10.0 %collective-permute-start = (f32[2,192,1]{2,1,0:T(8,128)S(1)}, f32[2,192,1]{2,1,0:T(8,128)S(1)}, u32[]{:S(2)}, u32[]{:S(2)}) collective-permute-start(f32[2,192,1]{2,1,0:T(8,128)S(1)} %get-tuple-element.329), channel_id=1, source_target_pairs={{8,0},{16,8},{24,16},{32,24},{40,32},{48,40},{56,48},{64,56},{72,6... | collective-permute-start | bytes 4616 | tf_op jit(solution)/shard_map/ppermute | solution.py:15
  162.2 10.3 %collective-permute-start.1 = (f32[2,192,1]{2,1,0:T(8,128)S(1)}, f32[2,192,1]{2,1,0:T(8,128)S(1)}, u32[]{:S(2)}, u32[]{:S(2)}) collective-permute-start(f32[2,192,1]{2,1,0:T(8,128)S(1)} %get-tuple-element.330), channel_id=1, source_target_pairs={{0,8},{8,16},{16,24},{24,32},{32,40},{40,48},{48,56},{56,64},{64,7... | collective-permute-start | bytes 4616 | tf_op jit(solution)/shard_map/ppermute | solution.py:14
  172.8 6.7 %copy-start.4 = (f32[128,128]{1,0:T(8,128)S(1)}, f32[128,128]{1,0:T(8,128)}, u32[]{:S(2)}) copy-start(f32[128,128]{1,0:T(8,128)} %param.29) | copy-start | bytes 196612
  172.8 6.7 %copy-start.7 = (f32[128]{0:T(128)S(1)}, f32[128]{0:T(128)}, u32[]{:S(2)}) copy-start(f32[128]{0:T(128)} %param.30) | copy-start | bytes 1540
  179.5 3.6 copy-start.9
  313.0 6.8 %collective-permute-start.2 = (f32[2,128]{1,0:T(2,128)S(1)}, f32[2,128]{1,0:T(2,128)S(1)}, u32[]{:S(2)}, u32[]{:S(2)}) collective-permute-start(f32[2,128]{1,0:T(2,128)S(1)} %bitcast_add_fusion.13), channel_id=1, source_target_pairs={{0,1},{1,2},{2,3},{3,4},{4,5},{5,6},{6,7},{8,9},{9,10},{10,11},{11... | collective-permute-start | bytes 3080 | tf_op jit(solution)/shard_map/ppermute | solution.py:23
  319.8 6.7 %collective-permute-start.3 = (f32[2,128]{1,0:T(2,128)S(1)}, f32[2,128]{1,0:T(2,128)S(1)}, u32[]{:S(2)}, u32[]{:S(2)}) collective-permute-start(f32[2,128]{1,0:T(2,128)S(1)} %bitcast_add_fusion.12), channel_id=1, source_target_pairs={{0,1},{1,2},{2,3},{3,4},{4,5},{5,6},{6,7},{8,9},{9,10},{10,11},{11... | collective-permute-start | bytes 3080 | tf_op jit(solution)/shard_map/ppermute | solution.py:23
  326.4 6.7 %collective-permute-start.4 = (f32[2,128]{1,0:T(2,128)S(1)}, f32[2,128]{1,0:T(2,128)S(1)}, u32[]{:S(2)}, u32[]{:S(2)}) collective-permute-start(f32[2,128]{1,0:T(2,128)S(1)} %bitcast_add_fusion.11), channel_id=1, source_target_pairs={{0,1},{1,2},{2,3},{3,4},{4,5},{5,6},{6,7},{8,9},{9,10},{10,11},{11... | collective-permute-start | bytes 3080 | tf_op jit(solution)/shard_map/ppermute | solution.py:23
  333.1 6.7 %collective-permute-start.5 = (f32[2,128]{1,0:T(2,128)S(1)}, f32[2,128]{1,0:T(2,128)S(1)}, u32[]{:S(2)}, u32[]{:S(2)}) collective-permute-start(f32[2,128]{1,0:T(2,128)S(1)} %bitcast_add_fusion.10), channel_id=1, source_target_pairs={{0,1},{1,2},{2,3},{3,4},{4,5},{5,6},{6,7},{8,9},{9,10},{10,11},{11... | collective-permute-start | bytes 3080 | tf_op jit(solution)/shard_map/ppermute | solution.py:23
  339.8 6.7 %collective-permute-start.6 = (f32[2,128]{1,0:T(2,128)S(1)}, f32[2,128]{1,0:T(2,128)S(1)}, u32[]{:S(2)}, u32[]{:S(2)}) collective-permute-start(f32[2,128]{1,0:T(2,128)S(1)} %bitcast_add_fusion.9), channel_id=1, source_target_pairs={{0,1},{1,2},{2,3},{3,4},{4,5},{5,6},{6,7},{8,9},{9,10},{10,11},{11... | collective-permute-start | bytes 3080 | tf_op jit(solution)/shard_map/ppermute | solution.py:23
  346.4 6.7 %collective-permute-start.7 = (f32[2,128]{1,0:T(2,128)S(1)}, f32[2,128]{1,0:T(2,128)S(1)}, u32[]{:S(2)}, u32[]{:S(2)}) collective-permute-start(f32[2,128]{1,0:T(2,128)S(1)} %bitcast_add_fusion.8), channel_id=1, source_target_pairs={{0,1},{1,2},{2,3},{3,4},{4,5},{5,6},{6,7},{8,9},{9,10},{10,11},{11... | collective-permute-start | bytes 3080 | tf_op jit(solution)/shard_map/ppermute | solution.py:23
  353.1 6.7 %collective-permute-start.8 = (f32[2,128]{1,0:T(2,128)S(1)}, f32[2,128]{1,0:T(2,128)S(1)}, u32[]{:S(2)}, u32[]{:S(2)}) collective-permute-start(f32[2,128]{1,0:T(2,128)S(1)} %bitcast_add_fusion.7), channel_id=1, source_target_pairs={{0,1},{1,2},{2,3},{3,4},{4,5},{5,6},{6,7},{8,9},{9,10},{10,11},{11... | collective-permute-start | bytes 3080 | tf_op jit(solution)/shard_map/ppermute | solution.py:23
  371.9 6.9 %collective-permute-start.9 = (f32[2,128]{1,0:T(2,128)S(1)}, f32[2,128]{1,0:T(2,128)S(1)}, u32[]{:S(2)}, u32[]{:S(2)}) collective-permute-start(f32[2,128]{1,0:T(2,128)S(1)} %bitcast_add_fusion.6), channel_id=1, source_target_pairs={{1,0},{2,1},{3,2},{4,3},{5,4},{6,5},{7,6},{9,8},{10,9},{11,10},{12... | collective-permute-start | bytes 3080 | tf_op jit(solution)/shard_map/ppermute | solution.py:23
  378.8 6.7 %collective-permute-start.10 = (f32[2,128]{1,0:T(2,128)S(1)}, f32[2,128]{1,0:T(2,128)S(1)}, u32[]{:S(2)}, u32[]{:S(2)}) collective-permute-start(f32[2,128]{1,0:T(2,128)S(1)} %bitcast_add_fusion.5), channel_id=1, source_target_pairs={{1,0},{2,1},{3,2},{4,3},{5,4},{6,5},{7,6},{9,8},{10,9},{11,10},{12... | collective-permute-start | bytes 3080 | tf_op jit(solution)/shard_map/ppermute | solution.py:23
  385.5 6.7 %collective-permute-start.11 = (f32[2,128]{1,0:T(2,128)S(1)}, f32[2,128]{1,0:T(2,128)S(1)}, u32[]{:S(2)}, u32[]{:S(2)}) collective-permute-start(f32[2,128]{1,0:T(2,128)S(1)} %bitcast_add_fusion.4), channel_id=1, source_target_pairs={{1,0},{2,1},{3,2},{4,3},{5,4},{6,5},{7,6},{9,8},{10,9},{11,10},{12... | collective-permute-start | bytes 3080 | tf_op jit(solution)/shard_map/ppermute | solution.py:23
  392.1 6.7 %collective-permute-start.12 = (f32[2,128]{1,0:T(2,128)S(1)}, f32[2,128]{1,0:T(2,128)S(1)}, u32[]{:S(2)}, u32[]{:S(2)}) collective-permute-start(f32[2,128]{1,0:T(2,128)S(1)} %bitcast_add_fusion.3), channel_id=1, source_target_pairs={{1,0},{2,1},{3,2},{4,3},{5,4},{6,5},{7,6},{9,8},{10,9},{11,10},{12... | collective-permute-start | bytes 3080 | tf_op jit(solution)/shard_map/ppermute | solution.py:23
  398.8 6.7 %collective-permute-start.13 = (f32[2,128]{1,0:T(2,128)S(1)}, f32[2,128]{1,0:T(2,128)S(1)}, u32[]{:S(2)}, u32[]{:S(2)}) collective-permute-start(f32[2,128]{1,0:T(2,128)S(1)} %bitcast_add_fusion.2), channel_id=1, source_target_pairs={{1,0},{2,1},{3,2},{4,3},{5,4},{6,5},{7,6},{9,8},{10,9},{11,10},{12... | collective-permute-start | bytes 3080 | tf_op jit(solution)/shard_map/ppermute | solution.py:23
  405.5 6.7 %collective-permute-start.14 = (f32[2,128]{1,0:T(2,128)S(1)}, f32[2,128]{1,0:T(2,128)S(1)}, u32[]{:S(2)}, u32[]{:S(2)}) collective-permute-start(f32[2,128]{1,0:T(2,128)S(1)} %bitcast_add_fusion.1), channel_id=1, source_target_pairs={{1,0},{2,1},{3,2},{4,3},{5,4},{6,5},{7,6},{9,8},{10,9},{11,10},{12... | collective-permute-start | bytes 3080 | tf_op jit(solution)/shard_map/ppermute | solution.py:23
  412.1 6.7 %collective-permute-start.15 = (f32[2,128]{1,0:T(2,128)S(1)}, f32[2,128]{1,0:T(2,128)S(1)}, u32[]{:S(2)}, u32[]{:S(2)}) collective-permute-start(f32[2,128]{1,0:T(2,128)S(1)} %bitcast_add_fusion), channel_id=1, source_target_pairs={{1,0},{2,1},{3,2},{4,3},{5,4},{6,5},{7,6},{9,8},{10,9},{11,10},{12... | collective-permute-start | bytes 3080 | tf_op jit(solution)/shard_map/ppermute | solution.py:23
where the time goes:
time: 420 us; the launch traced here: 419 us
  other arithmetic  144 us (34%)
  local copies, waits for them, and re-layouts  127 us (30%)
  starting transfers between devices  70.8 us (17%)
  waiting for transfers between devices  50.4 us (12%)
  matrix products  14.2 us (3%)
  loops' own time  11.7 us (3%)
    scatter-add x1, other arithmetic, local(): jax.ops.segment_sum(stress_flat, face_index, face_count + 1)[:face_count]  57 us
    scatter-add x1, other arithmetic, local(): jax.ops.segment_sum(jnp.ones_like(stress_flat), face_index, face_count + 1)  57 us
    ppermute x14, starting transfers between devices, shifted(): return lax.ppermute(shard, axis, pairs)  51.1 us
    ppermute x14, waiting for transfers between devices, shifted(): return lax.ppermute(shard, axis, pairs)  42.4 us
    gather x1, local copies, waits for them, and re-layouts, sample_at(): velocity_u[plane_idx, level_idx, span_idx]  32.9 us
    gather x1, local copies, waits for them, and re-layouts, sample_at(): velocity_v[plane_idx, level_idx, span_idx]  32.9 us
    gather x1, local copies, waits for them, and re-layouts, sample_at(): velocity_w[plane_idx, level_idx, span_idx]  32.9 us
    unnamed x27, local copies, waits for them, and re-layouts  19.3 us
  transfers between devices with their start and end apart: 17, of which 16 were waited for; matrix products, arithmetic and copies ran while one was open for 0% of the time, Pallas kernels for 0%

commit v1 on v0

v1 whole, which is shorter than its diff:
```python
import functools

import jax
import jax.numpy as jnp
from jax import lax
from jax.experimental import pallas as pl
from jax.experimental.pallas import tpu as pltpu
from jax.sharding import PartitionSpec as P

MESH = pl.DeviceIdType.MESH
LANES = 128
SUB = 8
WIN = 16
HMAX = 8
KB = 512
F32 = jnp.float32
BF16 = jnp.bfloat16


def load_rows(ref, p, b, steps):
    return ref[p, pl.ds(b, SUB, stride=steps), :]


def step_loop(count, unroll, body, init):
    def outer(i, carry):
        for j in range(unroll):
            carry = body(i * unroll + j, carry)
        return carry

    return lax.fori_loop(0, count // unroll, outer, init)


def kernel(
    gz,
    gy,
    nx,
    u_hbm,
    v_hbm,
    w_hbm,
    s_hbm,
    w_in_hbm,
    b_in_hbm,
    w_mid_hbm,
    b_mid_hbm,
    w_out_hbm,
    cell_hbm,
    height_hbm,
    face_hbm,
    owner_hbm,
    bl_out,
    q_out,
    fb_out,
    f_out,
    b_out,
    u_ref,
    s_ref,
    win_ref,
    w_in_ref,
    vec_ref,
    w_mid_ref,
    cell_ref,
    height_ref,
    face_ref,
    owner_ref,
    cols_ref,
    wl_ref,
    samp_ref,
    table_ref,
    acc_ref,
    keep_ref,
    gain_ref,
    gsrc_ref,
    lf_ref,
    ff_ref,
    bl_ref,
    q_ref,
    fb_ref,
    edge_ref,
    pack_ref,
    halo_ref,
    send_a,
    recv_a,
    send_b,
    recv_b,
    send_s,
    recv_s,
    load_sem,
    out_sem,
    halo_send,
    halo_recv,
    a_send,
    a_recv,
    b_send,
    b_recv,
    s_send,
    s_recv,
):
    planes, levels, _ = u_ref.shape
    steps = levels // SUB
    total_steps = planes * steps
    nyc = gz // nx
    roles = (0, 1, gy - 2, gy - 1)
    me = lax.axis_index("gz")
    level = lax.axis_index("gy")
    xx = me // nyc
    yc = me % nyc
    is_top = level >= gy // 2
    is_tot = (level == 0) | (level == gy - 1)
    is_role = is_tot | (level == 1) | (level == gy - 2)
    role = jnp.where(is_top, level - (gy - 4), level)

    start = pl.multiple_of(jnp.where(is_top, levels - WIN, 0), 8)
    load_u = pltpu.make_async_copy(u_hbm, u_ref, load_sem.at[0])
    load_s = pltpu.make_async_copy(s_hbm, s_ref, load_sem.at[1])
    lists = [
        pltpu.make_async_copy(src, dst, load_sem.at[2 + i])
        for i, (src, dst) in enumerate(
            [(cell_hbm, cell_ref), (height_hbm, height_ref), (face_hbm, face_ref), (owner_hbm, owner_ref)]
        )
    ]
    weights = [
        pltpu.make_async_copy(src, dst, load_sem.at[6 + i])
        for i, (src, dst) in enumerate(
            [
                (w_in_hbm, w_in_ref),
                (b_in_hbm, vec_ref.at[0]),
                (b_mid_hbm, vec_ref.at[1]),
                (w_out_hbm, vec_ref.at[2]),
                (w_mid_hbm, w_mid_ref),
                (v_hbm.at[:, pl.ds(start, WIN), :], win_ref.at[0]),
                (w_hbm.at[:, pl.ds(start, WIN), :], win_ref.at[1]),
            ]
        )
    ]
    load_u.start()

    @pl.when(is_tot)
    def _():
        for copy in weights:
            copy.start()

    @pl.when(is_role)
    def _():
        for copy in lists:
            copy.start()

    load_s.start()

    barrier = pltpu.get_barrier_semaphore()

    def greet(z, y):
        pl.semaphore_signal(barrier, inc=1, device_id=(z, y), device_id_type=MESH)

    left, right = lax.rem(me + gz - 1, gz), lax.rem(me + 1, gz)
    greet(left, level)
    greet(right, level)

    @pl.loop(1, gy)
    def _(d):
        greet(me, lax.rem(level + d, gy))

    @pl.loop(1, nx)
    def _(d):
        for r in roles:
            greet(lax.rem(xx + d, nx) * nyc + yc, r)

    @pl.when(is_role)
    def _():
        @pl.loop(1, nyc)
        def _(d):
            greet(xx * nyc + lax.rem(yc + d, nyc), level)

    lane = lax.broadcasted_iota(jnp.int32, (SUB, LANES), 1)
    row = lax.broadcasted_iota(jnp.int32, (SUB, LANES), 0)
    load_u.wait()
    packed = jnp.zeros((SUB, LANES), F32)
    for p in range(planes):

        def pack(b, acc, p=p):
            i = p * steps + b
            return jnp.where(lane // 2 == i, pltpu.roll(load_rows(u_ref, p, b, steps), 2 * i + 1, 1), acc)

        packed = step_loop(steps, 8, pack, packed)
    pack_ref[...] = packed

    base = gy - 1 + 2

    @pl.when(is_role)
    def _():
        pl.semaphore_wait(barrier, base + nyc - 1 + (nx - 1) * gy)

    @pl.when(jnp.logical_not(is_role))
    def _():
        pl.semaphore_wait(barrier, base)

    halo_copies = [
        pltpu.make_async_remote_copy(
            src_ref=pack_ref,
            dst_ref=halo_ref.at[slot],
            send_sem=halo_send.at[slot],
            recv_sem=halo_recv.at[slot],
            device_id=(z, level),
            device_id_type=MESH,
        )
        for slot, z in ((0, right), (1, left))
    ]
    for copy in halo_copies:
        copy.start()

    def copy_a(z, slot):
        return pltpu.make_async_remote_copy(
            src_ref=send_a.at[z],
            dst_ref=recv_a.at[slot],
            send_sem=a_send,
            recv_sem=a_recv,
            device_id=(xx * nyc + z, level),
            device_id_type=MESH,
        )

    def copy_b(x, y):
        return pltpu.make_async_remote_copy(
            src_ref=send_b.at[x],
            dst_ref=recv_b.at[role * nx + xx],
            send_sem=b_send,
            recv_sem=b_recv,
            device_id=(x * nyc + yc, y),
            device_id_type=MESH,
        )

    def copy_s(y):
        return pltpu.make_async_remote_copy(
            src_ref=send_s,
            dst_ref=recv_s.at[level],
            send_sem=s_send,
            recv_sem=s_recv,
            device_id=(me, y),
            device_id_type=MESH,
        )

    @pl.when(is_tot)
    def _():
        for copy in weights:
            copy.wait()
        vectors = jnp.concatenate(
            [w_in_ref[...], vec_ref[0], vec_ref[1], vec_ref[2], jnp.zeros((2, LANES), F32)], axis=0
        )
        columns = vectors.T
        for c in range(6):
            cols_ref[c] = jnp.broadcast_to(columns[:, c : c + 1], (LANES, LANES))
        mid = w_mid_ref[...].T
        mid_hi = mid.astype(BF16)
        mid_lo = (mid - mid_hi.astype(F32)).astype(BF16)
        wl_ref[...] = jnp.concatenate(
            [jnp.concatenate([mid_hi, mid_hi], axis=1), jnp.concatenate([mid_lo, mid_lo], axis=1)], axis=0
        )
        for p in range(planes):
            samp_ref[0, p * HMAX : (p + 1) * HMAX, :] = jnp.where(
                is_top, u_ref[p, levels - 1 - HMAX : levels - 1, :], u_ref[p, 1 : 1 + HMAX, :]
            )
            for c in range(2):
                samp_ref[1 + c, p * HMAX : (p + 1) * HMAX, :] = jnp.where(
                    is_top, win_ref[c, p, WIN - 1 - HMAX : WIN - 1, :], win_ref[c, p, 1 : 1 + HMAX, :]
                )

        @pl.loop(0, planes * HMAX // 2)
        def _(i):
            halves = []
            for h in range(2):
                k = i * 2 + h
                pre = cols_ref[3]
                for c in range(3):
                    pre = pre + cols_ref[c] * samp_ref[c, pl.ds(k, 1), :]
                hidden = jnp.tanh(pre)
                upper = hidden.astype(BF16)
                lower = (hidden - upper.astype(F32)).astype(BF16)
                halves.append(jnp.concatenate([upper, lower], axis=0))
            mixed = jnp.dot(wl_ref[...], jnp.concatenate(halves, axis=1), preferred_element_type=F32)
            for h in range(2):
                part = mixed[:, h * LANES : (h + 1) * LANES]
                second = jnp.tanh(part[:LANES] + part[LANES:] + cols_ref[4])
                table_ref[pl.ds(i * 2 + h, 1), :] = jnp.sum(second * cols_ref[5], axis=0, keepdims=True)

    @pl.when(is_role & jnp.logical_not(is_tot))
    def _():
        table_ref[...] = jnp.ones_like(table_ref)

    @pl.when(is_role)
    def _():
        for copy in lists:
            copy.wait()
        rows = cell_ref.shape[1]
        acc_ref[...] = jnp.zeros_like(acc_ref)
        bins = acc_ref.shape[0]
        rows_iota = lax.broadcasted_iota(jnp.int32, (LANES, KB), 0)
        bins_iota = lax.broadcasted_iota(jnp.int32, (bins, KB), 0)

        @pl.loop(0, rows // KB)
        def _(i):
            at = pl.ds(pl.multiple_of(i * KB, KB), KB)

            def wall(ref):
                return jnp.where(is_top, ref[1:2, at], ref[0:1, at])

            cell, height, face = wall(cell_ref), wall(height_ref), wall(face_ref)
            owner = owner_ref[:, pl.ds(pl.multiple_of(jnp.where(is_top, rows, 0) + i * KB, KB), KB)]
            span = cell % LANES
            key = (cell // LANES) * HMAX + jnp.where(is_top, HMAX - height, height - 1)
            picks = []
            for j in range(KB // LANES):
                cut = slice(j * LANES, (j + 1) * LANES)
                index = jnp.broadcast_to(span[:, cut], (SUB, LANES))
                keyed = jnp.broadcast_to(key[:, cut], (SUB, LANES))
                value = jnp.zeros((SUB, LANES), F32)
                for t in range(planes):
                    got = jnp.take_along_axis(table_ref[t * HMAX : (t + 1) * HMAX, :], index, axis=1)
                    value = value + jnp.where(keyed == row + t * HMAX, got, 0.0)
                picks.append(jnp.sum(value, axis=0, keepdims=True))
            value = jnp.concatenate(picks, axis=1)
            first = value.astype(BF16).astype(F32)
            rest = value - first
            low = face % LANES
            high = (owner % nyc) * (2 * nx) + (owner // nyc) * 2 + face // LANES
            onto = jnp.where(bins_iota == high, 1.0, 0.0).astype(BF16)
            named = rows_iota == low
            carried = jnp.concatenate(
                [jnp.where(named, first, 0.0).astype(BF16), jnp.where(named, rest, 0.0).astype(BF16)], axis=0
            )
            acc_ref[...] += lax.dot_general(
                onto, carried, (((1,), (1,)), ((), ())), preferred_element_type=F32
            )

        binned = acc_ref[:, :LANES] + acc_ref[:, LANES:]
        send_a[...] = binned.reshape(send_a.shape)
        recv_a[yc] = send_a[yc]

        @pl.loop(1, nyc)
        def _(d):
            copy_a(lax.rem(yc + d, nyc), yc).start()

    load_s.wait()
    for copy in halo_copies:
        copy.wait_recv()
    merged = jnp.where(lane % 2 == 1, pltpu.roll(halo_ref[0], 1, 1), pltpu.roll(halo_ref[1], LANES - 1, 1))
    zero, one = jnp.zeros((SUB, LANES), F32), jnp.ones((SUB, LANES), F32)
    summaries = []
    for p in range(planes):

        def prepare(b, _, p=p):
            i = p * steps + b
            stiff = load_rows(s_ref, p, b, steps)
            here = load_rows(u_ref, p, b, steps)
            halo = pltpu.roll(merged, LANES - 1 - 2 * i, 1)
            before = jnp.where(lane == 0, halo, pltpu.roll(here, 1, 1))
            after = jnp.where(lane == LANES - 1, halo, pltpu.roll(here, LANES - 1, 1))
            source = here + 0.2 * (after + before - 2.0 * here)
            gain = 1.0 / (1.0 + stiff)
            keep_ref[p, b] = stiff * gain
            gain_ref[p, b] = gain
            gsrc_ref[p, b] = gain * source
            return _

        step_loop(steps, 4, prepare, 0)

    def forward(b, carry):
        out = []
        for p in range(planes):
            value, factor = carry[2 * p : 2 * p + 2]
            keep = keep_ref[p, b]
            value = keep * value + gsrc_ref[p, b]
            factor = keep * factor
            lf_ref[p, b] = value
            ff_ref[p, b] = factor
            out += [value, factor]
        return tuple(out)

    forwards = step_loop(steps, 4, forward, (zero, one) * planes)

    def backward(t, carry):
        out = []
        b = steps - 1 - t
        for p in range(planes):
            value, response, factor = carry[3 * p : 3 * p + 3]
            keep, gain = keep_ref[p, b], gain_ref[p, b]
            value = keep * value + gain * lf_ref[p, b]
            response = keep * response + gain * ff_ref[p, b]
            factor = keep * factor
            at = pl.ds(b, SUB, stride=steps)
            bl_ref[p, at, :] = value
            q_ref[p, at, :] = response
            fb_ref[p, at, :] = factor
            out += [value, response, factor]
        return tuple(out)

    backwards = step_loop(steps, 4, backward, (zero, zero, one) * planes)
    outs = [
        pltpu.make_async_copy(src, dst, out_sem.at[i])
        for i, (src, dst) in enumerate([(bl_ref, bl_out), (q_ref, q_out), (fb_ref, fb_out)])
    ]
    for copy in outs:
        copy.start()

    inner = []
    for p in range(planes):
        local_f = forwards[2 * p]
        local_b, response, product = backwards[3 * p : 3 * p + 3]
        pi, li = product, local_f
        for d in (1, 2, 4):
            ok = row >= d
            lp = jnp.where(ok, pltpu.roll(li, d, 0), 0.0)
            pp = jnp.where(ok, pltpu.roll(pi, d, 0), 1.0)
            li, pi = pi * lp + li, pi * pp
        pf = jnp.where(row >= 1, pltpu.roll(pi, 1, 0), 1.0)
        lf = jnp.where(row >= 1, pltpu.roll(li, 1, 0), 0.0)
        pb, cb, qb = product, local_b + response * lf, response * pf
        for d in (1, 2, 4):
            ok = row < SUB - d
            cp = jnp.where(ok, pltpu.roll(cb, SUB - d, 0), 0.0)
            qp = jnp.where(ok, pltpu.roll(qb, SUB - d, 0), 0.0)
            pp = jnp.where(ok, pltpu.roll(pb, SUB - d, 0), 1.0)
            cb, qb, pb = pb * cp + cb, pb * qp + qb, pb * pp
        ok = row < SUB - 1
        summaries.append((pb[0:1], li[SUB - 1 : SUB], cb[0:1], qb[0:1]))
        inner.append(
            (
                pf,
                lf,
                jnp.where(ok, pltpu.roll(pb, SUB - 1, 0), 1.0),
                jnp.where(ok, pltpu.roll(cb, SUB - 1, 0), 0.0),
                jnp.where(ok, pltpu.roll(qb, SUB - 1, 0), 0.0),
            )
        )
    own_alpha = jnp.concatenate([1.0 / keep_ref[p, 0, 0:1] for p in range(planes)], axis=0)
    own_eps = jnp.concatenate([1.0 / s_ref[p, levels - 1 : levels, :] for p in range(planes)], axis=0)
    at_bottom, at_top = level == 0, level == gy - 1
    blocks = [jnp.concatenate([summaries[p][c] for p in range(planes)], axis=0) for c in range(4)]
    blocks[0] = blocks[0] * jnp.where(at_bottom, own_alpha, jnp.where(at_top, own_eps, 1.0))
    summary = jnp.concatenate(blocks, axis=0)
    send_s[...] = summary
    recv_s[level] = summary

    @pl.loop(1, gy)
    def _(d):
        copy_s(lax.rem(level + d, gy)).start()

    @pl.when(is_role)
    def _():
        pltpu.make_async_copy(recv_a.at[pl.ds(0, nyc - 1)], recv_a.at[pl.ds(0, nyc - 1)], a_recv).wait()
        part = recv_a[0]
        for i in range(1, nyc):
            part = part + recv_a[i]
        for x in range(nx):
            send_b[x] = part[2 * x : 2 * x + 2, :]
        recv_b[role * nx + xx] = send_b[xx]

        @pl.loop(1, nx * gy)
        def _(d):
            flat = lax.rem(xx * gy + level + d, nx * gy)
            copy_b(flat // gy, flat % gy).start()

    pltpu.make_async_copy(recv_s.at[pl.ds(0, gy - 1)], recv_s.at[pl.ds(0, gy - 1)], s_recv).wait()

    def block(g, c):
        return recv_s[g, 2 * c : 2 * c + 2, :]

    alphas, betas = [None, block(0, 0)], [None, block(0, 1)]
    for g in range(1, gy - 1):
        alphas.append(block(g, 0) * alphas[g])
        betas.append(block(g, 0) * betas[g] + block(g, 1))
    alpha, beta = jnp.where(at_bottom, own_alpha, 0.0), jnp.zeros_like(own_alpha)
    for g in range(1, gy):
        alpha = jnp.where(level == g, alphas[g], alpha)
        beta = jnp.where(level == g, betas[g], beta)
    top = gy - 1
    gam, dlt, eps = block(top, 3) * alphas[top], block(top, 2) + block(top, 3) * betas[top], block(top, 0)
    gamma, delta = jnp.zeros_like(own_alpha), jnp.zeros_like(own_alpha)
    epsilon = jnp.where(at_top, own_eps, 0.0)
    for g in range(gy - 2, -1, -1):
        gamma = jnp.where(level == g, gam, gamma)
        delta = jnp.where(level == g, dlt, delta)
        epsilon = jnp.where(level == g, eps, epsilon)
        if g:
            gam = block(g, 0) * gam + block(g, 3) * alphas[g]
            dlt = block(g, 0) * dlt + block(g, 2) + block(g, 3) * betas[g]
            eps = block(g, 0) * eps

    count = 4 * nx

    @pl.when(is_role)
    def _():
        pltpu.make_async_copy(recv_b.at[pl.ds(0, count - 1)], recv_b.at[pl.ds(0, count - 1)], b_recv).wait()

    @pl.when(jnp.logical_not(is_role))
    def _():
        pltpu.make_async_copy(recv_b, recv_b, b_recv).wait()

    sums = []
    for r in range(4):
        total = recv_b[r * nx]
        for x in range(1, nx):
            total = total + recv_b[r * nx + x]
        sums.append(total)
    stress_low = sums[0] / jnp.maximum(sums[1], 1.0)
    stress_top = sums[3] / jnp.maximum(sums[2], 1.0)
    f_in = alpha * stress_low + beta
    b_in = gamma * stress_low + delta + epsilon * stress_top
    for p in range(planes):
        pf, lf, pb, cb, qb = inner[p]
        edge_ref[0, p] = pf * f_in[p : p + 1] + lf
        edge_ref[1, p] = pb * b_in[p : p + 1] + cb + qb * f_in[p : p + 1]
    edges = [
        pltpu.make_async_copy(edge_ref.at[i], dst, out_sem.at[3 + i]) for i, dst in enumerate([f_out, b_out])
    ]
    for copy in edges:
        copy.start()

    for copy in halo_copies:
        copy.wait_send()
    pltpu.make_async_copy(recv_s.at[pl.ds(0, gy - 1)], recv_s.at[pl.ds(0, gy - 1)], s_send).wait()

    @pl.when(is_role)
    def _():
        pltpu.make_async_copy(send_a.at[pl.ds(0, nyc - 1)], send_a.at[pl.ds(0, nyc - 1)], a_send).wait()
        for _ in range(gy - 1):
            pltpu.make_async_copy(send_b, send_b, b_send).wait()
        pltpu.make_async_copy(send_b.at[pl.ds(0, nx - 1)], send_b.at[pl.ds(0, nx - 1)], b_send).wait()

    for copy in outs + edges:
        copy.wait()


def local(gz, gy, nx, *args):
    u, v, w, s, w_in, b_in, w_mid, b_mid, w_out, cell, height, face, owner = args
    planes, levels, span = u.shape
    steps = levels // SUB
    nyc = gz // nx
    rows = cell.shape[1]
    field = jax.ShapeDtypeStruct(u.shape, F32)
    vmem = pltpu.VMEM
    scratch = [
        vmem(u.shape, F32),
        vmem(u.shape, F32),
        vmem((2, planes, WIN, span), F32),
        vmem((3, span), F32),
        vmem((3, 1, span), F32),
        vmem((span, span), F32),
        vmem((2, rows), jnp.int32),
        vmem((2, rows), jnp.int32),
        vmem((2, rows), jnp.int32),
        vmem((1, 2 * rows), jnp.int32),
        vmem((6, span, span), F32),
        vmem((2 * span, 2 * span), BF16),
        vmem((3, planes * HMAX, span), F32),
        vmem((planes * HMAX, span), F32),
        vmem((2 * gz, 2 * span), F32),
        vmem((planes, steps, SUB, span), F32),
        vmem((planes, steps, SUB, span), F32),
        vmem((planes, steps, SUB, span), F32),
        vmem((planes, steps, SUB, span), F32),
        vmem((planes, steps, SUB, span), F32),
        vmem(u.shape, F32),
        vmem(u.shape, F32),
        vmem(u.shape, F32),
        vmem((2, planes, SUB, span), F32),
        vmem((SUB, span), F32),
        vmem((2, SUB, span), F32),
        vmem((nyc, 2 * nx, span), F32),
        vmem((nyc, 2 * nx, span), F32),
        vmem((nx, 2, span), F32),
        vmem((4 * nx, 2, span), F32),
        vmem((8, span), F32),
        vmem((gy, 8, span), F32),
        pltpu.SemaphoreType.DMA((13,)),
        pltpu.SemaphoreType.DMA((5,)),
        pltpu.SemaphoreType.DMA((2,)),
        pltpu.SemaphoreType.DMA((2,)),
    ] + [pltpu.SemaphoreType.DMA] * 6
    bl, q, fb, below, above = pl.pallas_call(
        functools.partial(kernel, gz, gy, nx),
        out_shape=[field] * 3 + [jax.ShapeDtypeStruct((planes, SUB, span), F32)] * 2,
        in_specs=[pl.BlockSpec(memory_space=pl.ANY)] * 13,
        out_specs=[pl.BlockSpec(memory_space=pl.ANY)] * 5,
        scratch_shapes=scratch,
        compiler_params=pltpu.CompilerParams(
            collective_id=0, has_side_effects=True, vmem_limit_bytes=63 * 2**20
        ),
    )(
        u,
        v,
        w,
        s,
        w_in,
        b_in[None, :],
        w_mid,
        b_mid[None, :],
        w_out[None, :],
        cell,
        height,
        face,
        owner.reshape(1, 2 * rows),
    )
    shape = (planes, SUB, steps, span)
    out = bl.reshape(shape) + q.reshape(shape) * below[:, :, None, :] + fb.reshape(shape) * above[:, :, None, :]
    return out.reshape(u.shape)


def solution(mesh):
    field = P(None, "gy", "gz")
    gz, gy = mesh.shape["gz"], mesh.shape["gy"]
    return jax.shard_map(
        functools.partial(local, gz, gy, 4),
        mesh=mesh,
        in_specs=(field,) * 4 + (P(),) * 5 + (P(None, "gz"),) * 3 + (P(None, "gz", None),),
        out_specs=field,
        check_vma=False,
    )
```

time: 420 us -> 32.6 us (0.08)
  the two profiles are of different devices: /device:TPU:192 before, /device:TPU:1 now
where the time goes in v1:
time: 32.6 us; the launch traced here: 32.4 us
  Pallas kernels  29.9 us (92%)
  other arithmetic  1.83 us (6%)
  local copies, waits for them, and re-layouts  0.69 us (2%)
    pallas_call x1, Pallas kernels, local(): pl.pallas_call(functools.partial(kernel, gz, gy, nx), out_shape=[field] *...  29.9 us
    add x1, other arithmetic, local(): bl.reshape(shape) + q.reshape(shape) * below[:, :, None, :]  1.83 us
    unnamed x2, local copies, waits for them, and re-layouts  0.69 us

profile of v1, /device:TPU:1, one launch (start us, length us, event | category | flops | bytes accessed | tf_op | source)
XLA Modules:
  0.0 32.4 jit_solution(13707633010860384074)
XLA Ops:
  0.0 29.9 %shard_map.127 = (f32[2,192,128]{2,1,0:T(8,128)}, f32[2,192,128]{2,1,0:T(8,128)}, f32[2,192,128]{2,1,0:T(8,128)}, f32[2,8,128]{2,1,0:T(8,128)}, f32[2,8,128]{2,1,0:T(8,128)}) custom-call(f32[2,192,128]{2,1,0:T(8,128)} %u_hbm.1, f32[2,192,128]{2,1,0:T(8,128)} %v_hbm.1, f32[2,192,128]{2,1,0:T(8,128)} %w_hbm.1, f32[2,192,128]{2,1,0:T(8,128)} %s_hbm.1, ...), custom_call_target="tpu_custom_call" | custom-call | tf_op jit(solution)/shard_map/pallas_call | solution.py:577
  29.9 0.0 copy-start
  29.9 0.7 %copy-done = f32[2,8,128]{2,1,0:T(8,128)S(1)} copy-done((f32[2,8,128]{2,1,0:T(8,128)S(1)}, f32[2,8,128]{2,1,0:T(8,128)}, u32[]{:S(2)}) %copy-start) | copy-done | bytes 8216
  30.6 1.8 %fusion = f32[2,192,128]{2,1,0:T(8,128)} fusion(f32[2,192,128]{2,1,0:T(8,128)} %get-tuple-element.13, f32[2,192,128]{2,1,0:T(8,128)} %get-tuple-element.10, f32[2,192,128]{2,1,0:T(8,128)} %get-tuple-element.11, f32[2,8,128]{2,1,0:T(8,128)} %get-tuple-element.14, f32[2,8,128]{2,1,0:T(8,128)S(1)} %copy-done), kind=kLoop, calls=%fused_computation.1 | loop fusion | flops 196608 | bytes 802816 | tf_op jit(solution)/shard_map/add | solution.py:602
Async XLA Ops:
  29.9 0.7 %copy-start = (f32[2,8,128]{2,1,0:T(8,128)S(1)}, f32[2,8,128]{2,1,0:T(8,128)}, u32[]{:S(2)}) copy-start(f32[2,8,128]{2,1,0:T(8,128)} %get-tuple-element.12) | copy-start | bytes 24580

commit v2 on v1

--- a/solution.py
+++ b/solution.py
@@ -12,7 +12,8 @@
 SUB = 8
 WIN = 16
 HMAX = 8
-KB = 512
+KB = 4096
+NK = 16
 F32 = jnp.float32
 BF16 = jnp.bfloat16
 
@@ -28,6 +29,93 @@
         return carry
 
     return lax.fori_loop(0, count // unroll, outer, init)
+
+
+def network(is_top, u_ref, win_ref, w_in_ref, vec_ref, w_mid_ref, cols_ref, wl_ref, samp_ref, table_ref):
+    planes, levels, _ = u_ref.shape
+    vectors = jnp.concatenate(
+        [w_in_ref[...], vec_ref[0], vec_ref[1], vec_ref[2], jnp.zeros((2, LANES), F32)], axis=0
+    )
+    columns = vectors.T
+    for c in range(6):
+        cols_ref[c] = jnp.broadcast_to(columns[:, c : c + 1], (LANES, LANES))
+    mid = w_mid_ref[...].T
+    mid_hi = mid.astype(BF16)
+    mid_lo = (mid - mid_hi.astype(F32)).astype(BF16)
+    wl_ref[...] = jnp.concatenate(
+        [jnp.concatenate([mid_hi, mid_hi], axis=1), jnp.concatenate([mid_lo, mid_lo], axis=1)], axis=0
+    )
+    for p in range(planes):
+        samp_ref[0, p * HMAX : (p + 1) * HMAX, :] = jnp.where(
+            is_top, u_ref[p, levels - 1 - HMAX : levels - 1, :], u_ref[p, 1 : 1 + HMAX, :]
+        )
+        for c in range(2):
+            samp_ref[1 + c, p * HMAX : (p + 1) * HMAX, :] = jnp.where(
+                is_top, win_ref[c, p, WIN - 1 - HMAX : WIN - 1, :], win_ref[c, p, 1 : 1 + HMAX, :]
+            )
+
+    @pl.loop(0, planes * HMAX // NK)
+    def _(i):
+        halves = []
+        for h in range(NK):
+            k = i * NK + h
+            pre = cols_ref[3]
+            for c in range(3):
+                pre = pre + cols_ref[c] * samp_ref[c, pl.ds(k, 1), :]
+            hidden = jnp.tanh(pre)
+            upper = hidden.astype(BF16)
+            lower = (hidden - upper.astype(F32)).astype(BF16)
+            halves.append(jnp.concatenate([upper, lower], axis=0))
+        mixed = jnp.dot(wl_ref[...], jnp.concatenate(halves, axis=1), preferred_element_type=F32)
+        for h in range(NK):
+            part = mixed[:, h * LANES : (h + 1) * LANES]
+            second = jnp.tanh(part[:LANES] + part[LANES:] + cols_ref[4])
+            table_ref[pl.ds(i * NK + h, 1), :] = jnp.sum(second * cols_ref[5], axis=0, keepdims=True)
+
+
+def binning(is_top, nx, nyc, cell_ref, height_ref, face_ref, owner_ref, table_ref, acc_ref):
+    rows = cell_ref.shape[1]
+    planes = table_ref.shape[0] // HMAX
+    acc_ref[...] = jnp.zeros_like(acc_ref)
+    bins = acc_ref.shape[0]
+    row = lax.broadcasted_iota(jnp.int32, (SUB, LANES), 0)
+    rows_iota = lax.broadcasted_iota(jnp.int32, (LANES, KB), 0)
+    bins_iota = lax.broadcasted_iota(jnp.int32, (bins, KB), 0)
+
+    @pl.loop(0, rows // KB)
+    def _(i):
+        at = pl.ds(pl.multiple_of(i * KB, KB), KB)
+
+        def wall(ref):
+            return jnp.where(is_top, ref[1:2, at], ref[0:1, at])
+
+        cell, height, face = wall(cell_ref), wall(height_ref), wall(face_ref)
+        owner = owner_ref[:, pl.ds(pl.multiple_of(jnp.where(is_top, rows, 0) + i * KB, KB), KB)]
+        span = cell % LANES
+        key = (cell // LANES) * HMAX + jnp.where(is_top, HMAX - height, height - 1)
+        picks = []
+        for j in range(KB // LANES):
+            cut = slice(j * LANES, (j + 1) * LANES)
+            index = jnp.broadcast_to(span[:, cut], (SUB, LANES))
+            keyed = jnp.broadcast_to(key[:, cut], (SUB, LANES))
+            value = jnp.zeros((SUB, LANES), F32)
+            for t in range(planes):
+                got = jnp.take_along_axis(table_ref[t * HMAX : (t + 1) * HMAX, :], index, axis=1)
+                value = value + jnp.where(keyed == row + t * HMAX, got, 0.0)
+            picks.append(jnp.sum(value, axis=0, keepdims=True))
+        value = jnp.concatenate(picks, axis=1)
+        first = value.astype(BF16).astype(F32)
+        rest = value - first
+        low = face % LANES
+        high = (owner % nyc) * (2 * nx) + (owner // nyc) * 2 + face // LANES
+        onto = jnp.where(bins_iota == high, 1.0, 0.0).astype(BF16)
+        named = rows_iota == low
+        carried = jnp.concatenate(
+            [jnp.where(named, first, 0.0).astype(BF16), jnp.where(named, rest, 0.0).astype(BF16)], axis=0
+        )
+        acc_ref[...] += lax.dot_general(
+            onto, carried, (((1,), (1,)), ((), ())), preferred_element_type=F32
+        )
 
 
 def kernel(
@@ -47,11 +135,7 @@
     height_hbm,
     face_hbm,
     owner_hbm,
-    bl_out,
-    q_out,
-    fb_out,
-    f_out,
-    b_out,
+    out_ref,
     u_ref,
     s_ref,
     win_ref,
@@ -75,7 +159,6 @@
     bl_ref,
     q_ref,
     fb_ref,
-    edge_ref,
     pack_ref,
     halo_ref,
     send_a,
@@ -85,7 +168,6 @@
     send_s,
     recv_s,
     load_sem,
-    out_sem,
     halo_send,
     halo_recv,
     a_send,
@@ -241,44 +323,7 @@
     def _():
         for copy in weights:
             copy.wait()
-        vectors = jnp.concatenate(
-            [w_in_ref[...], vec_ref[0], vec_ref[1], vec_ref[2], jnp.zeros((2, LANES), F32)], axis=0
-        )
-        columns = vectors.T
-        for c in range(6):
-            cols_ref[c] = jnp.broadcast_to(columns[:, c : c + 1], (LANES, LANES))
-        mid = w_mid_ref[...].T
-        mid_hi = mid.astype(BF16)
-        mid_lo = (mid - mid_hi.astype(F32)).astype(BF16)
-        wl_ref[...] = jnp.concatenate(
-            [jnp.concatenate([mid_hi, mid_hi], axis=1), jnp.concatenate([mid_lo, mid_lo], axis=1)], axis=0
-        )
-        for p in range(planes):
-            samp_ref[0, p * HMAX : (p + 1) * HMAX, :] = jnp.where(
-                is_top, u_ref[p, levels - 1 - HMAX : levels - 1, :], u_ref[p, 1 : 1 + HMAX, :]
-            )
-            for c in range(2):
-                samp_ref[1 + c, p * HMAX : (p + 1) * HMAX, :] = jnp.where(
-                    is_top, win_ref[c, p, WIN - 1 - HMAX : WIN - 1, :], win_ref[c, p, 1 : 1 + HMAX, :]
-                )
-
-        @pl.loop(0, planes * HMAX // 2)
-        def _(i):
-            halves = []
-            for h in range(2):
-                k = i * 2 + h
-                pre = cols_ref[3]
-                for c in range(3):
-                    pre = pre + cols_ref[c] * samp_ref[c, pl.ds(k, 1), :]
-                hidden = jnp.tanh(pre)
-                upper = hidden.astype(BF16)
-                lower = (hidden - upper.astype(F32)).astype(BF16)
-                halves.append(jnp.concatenate([upper, lower], axis=0))
-            mixed = jnp.dot(wl_ref[...], jnp.concatenate(halves, axis=1), preferred_element_type=F32)
-            for h in range(2):
-                part = mixed[:, h * LANES : (h + 1) * LANES]
-                second = jnp.tanh(part[:LANES] + part[LANES:] + cols_ref[4])
-                table_ref[pl.ds(i * 2 + h, 1), :] = jnp.sum(second * cols_ref[5], axis=0, keepdims=True)
+        network(is_top, u_ref, win_ref, w_in_ref, vec_ref, w_mid_ref, cols_ref, wl_ref, samp_ref, table_ref)
 
     @pl.when(is_role & jnp.logical_not(is_tot))
     def _():
@@ -288,53 +333,12 @@
     def _():
         for copy in lists:
             copy.wait()
-        rows = cell_ref.shape[1]
-        acc_ref[...] = jnp.zeros_like(acc_ref)
-        bins = acc_ref.shape[0]
-        rows_iota = lax.broadcasted_iota(jnp.int32, (LANES, KB), 0)
-        bins_iota = lax.broadcasted_iota(jnp.int32, (bins, KB), 0)
-
-        @pl.loop(0, rows // KB)
-        def _(i):
-            at = pl.ds(pl.multiple_of(i * KB, KB), KB)
-
-            def wall(ref):
-                return jnp.where(is_top, ref[1:2, at], ref[0:1, at])
-
-            cell, height, face = wall(cell_ref), wall(height_ref), wall(face_ref)
-            owner = owner_ref[:, pl.ds(pl.multiple_of(jnp.where(is_top, rows, 0) + i * KB, KB), KB)]
-            span = cell % LANES
-            key = (cell // LANES) * HMAX + jnp.where(is_top, HMAX - height, height - 1)
-            picks = []
-            for j in range(KB // LANES):
-                cut = slice(j * LANES, (j + 1) * LANES)
-                index = jnp.broadcast_to(span[:, cut], (SUB, LANES))
-                keyed = jnp.broadcast_to(key[:, cut], (SUB, LANES))
-                value = jnp.zeros((SUB, LANES), F32)
-                for t in range(planes):
-                    got = jnp.take_along_axis(table_ref[t * HMAX : (t + 1) * HMAX, :], index, axis=1)
-                    value = value + jnp.where(keyed == row + t * HMAX, got, 0.0)
-                picks.append(jnp.sum(value, axis=0, keepdims=True))
-            value = jnp.concatenate(picks, axis=1)
-            first = value.astype(BF16).astype(F32)
-            rest = value - first
-            low = face % LANES
-            high = (owner % nyc) * (2 * nx) + (owner // nyc) * 2 + face // LANES
-            onto = jnp.where(bins_iota == high, 1.0, 0.0).astype(BF16)
-            named = rows_iota == low
-            carried = jnp.concatenate(
-                [jnp.where(named, first, 0.0).astype(BF16), jnp.where(named, rest, 0.0).astype(BF16)], axis=0
-            )
-            acc_ref[...] += lax.dot_general(
-                onto, carried, (((1,), (1,)), ((), ())), preferred_element_type=F32
-            )
-
+        binning(is_top, nx, nyc, cell_ref, height_ref, face_ref, owner_ref, table_ref, acc_ref)
         binned = acc_ref[:, :LANES] + acc_ref[:, LANES:]
         send_a[...] = binned.reshape(send_a.shape)
         recv_a[yc] = send_a[yc]
 
-        @pl.loop(1, nyc)
-        def _(d):
+        for d in sorted(range(1, nyc), key=lambda d: -min(d, nyc - d)):
             copy_a(lax.rem(yc + d, nyc), yc).start()
 
     load_s.wait()
@@ -384,20 +388,13 @@
             value = keep * value + gain * lf_ref[p, b]
             response = keep * response + gain * ff_ref[p, b]
             factor = keep * factor
-            at = pl.ds(b, SUB, stride=steps)
-            bl_ref[p, at, :] = value
-            q_ref[p, at, :] = response
-            fb_ref[p, at, :] = factor
+            bl_ref[p, b] = value
+            q_ref[p, b] = response
+            fb_ref[p, b] = factor
             out += [value, response, factor]
         return tuple(out)
 
     backwards = step_loop(steps, 4, backward, (zero, zero, one) * planes)
-    outs = [
-        pltpu.make_async_copy(src, dst, out_sem.at[i])
-        for i, (src, dst) in enumerate([(bl_ref, bl_out), (q_ref, q_out), (fb_ref, fb_out)])
-    ]
-    for copy in outs:
-        copy.start()
 
     inner = []
     for p in range(planes):
@@ -452,10 +449,13 @@
             send_b[x] = part[2 * x : 2 * x + 2, :]
         recv_b[role * nx + xx] = send_b[xx]
 
-        @pl.loop(1, nx * gy)
-        def _(d):
-            flat = lax.rem(xx * gy + level + d, nx * gy)
-            copy_b(flat // gy, flat % gy).start()
+        for y in range(gy):
+            for d in sorted(range(1, nx), key=lambda d: -min(d, nx - d)):
+                copy_b(lax.rem(xx + d, nx), y).start()
+
+            @pl.when(level != y)
+            def _(y=y):
+                copy_b(xx, y).start()
 
     pltpu.make_async_copy(recv_s.at[pl.ds(0, gy - 1)], recv_s.at[pl.ds(0, gy - 1)], s_recv).wait()
 
@@ -505,13 +505,14 @@
     b_in = gamma * stress_low + delta + epsilon * stress_top
     for p in range(planes):
         pf, lf, pb, cb, qb = inner[p]
-        edge_ref[0, p] = pf * f_in[p : p + 1] + lf
-        edge_ref[1, p] = pb * b_in[p : p + 1] + cb + qb * f_in[p : p + 1]
-    edges = [
-        pltpu.make_async_copy(edge_ref.at[i], dst, out_sem.at[3 + i]) for i, dst in enumerate([f_out, b_out])
-    ]
-    for copy in edges:
-        copy.start()
+        below = pf * f_in[p : p + 1] + lf
+        above = pb * b_in[p : p + 1] + cb + qb * f_in[p : p + 1]
+
+        def finish(b, _, p=p, below=below, above=above):
+            out_ref[p, pl.ds(b, SUB, stride=steps), :] = bl_ref[p, b] + q_ref[p, b] * below + fb_ref[p, b] * above
+            return _
+
+        step_loop(steps, steps, finish, 0)
 
     for copy in halo_copies:
         copy.wait_send()
@@ -523,9 +524,6 @@
         for _ in range(gy - 1):
             pltpu.make_async_copy(send_b, send_b, b_send).wait()
         pltpu.make_async_copy(send_b.at[pl.ds(0, nx - 1)], send_b.at[pl.ds(0, nx - 1)], b_send).wait()
-
-    for copy in outs + edges:
-        copy.wait()
 
 
 def local(gz, gy, nx, *args):
@@ -534,7 +532,6 @@
     steps = levels // SUB
     nyc = gz // nx
     rows = cell.shape[1]
-    field = jax.ShapeDtypeStruct(u.shape, F32)
     vmem = pltpu.VMEM
     scratch = [
         vmem(u.shape, F32),
@@ -557,10 +554,9 @@
         vmem((planes, steps, SUB, span), F32),
         vmem((planes, steps, SUB, span), F32),
         vmem((planes, steps, SUB, span), F32),
-        vmem(u.shape, F32),
-        vmem(u.shape, F32),
-        vmem(u.shape, F32),
-        vmem((2, planes, SUB, span), F32),
+        vmem((planes, steps, SUB, span), F32),
+        vmem((planes, steps, SUB, span), F32),
+        vmem((planes, steps, SUB, span), F32),
         vmem((SUB, span), F32),
         vmem((2, SUB, span), F32),
         vmem((nyc, 2 * nx, span), F32),
@@ -570,20 +566,10 @@
         vmem((8, span), F32),
         vmem((gy, 8, span), F32),
         pltpu.SemaphoreType.DMA((13,)),
-        pltpu.SemaphoreType.DMA((5,)),
         pltpu.SemaphoreType.DMA((2,)),
         pltpu.SemaphoreType.DMA((2,)),
     ] + [pltpu.SemaphoreType.DMA] * 6
-    bl, q, fb, below, above = pl.pallas_call(
-        functools.partial(kernel, gz, gy, nx),
-        out_shape=[field] * 3 + [jax.ShapeDtypeStruct((planes, SUB, span), F32)] * 2,
-        in_specs=[pl.BlockSpec(memory_space=pl.ANY)] * 13,
-        out_specs=[pl.BlockSpec(memory_space=pl.ANY)] * 5,
-        scratch_shapes=scratch,
-        compiler_params=pltpu.CompilerParams(
-            collective_id=0, has_side_effects=True, vmem_limit_bytes=63 * 2**20
-        ),
-    )(
+    operands = [
         u,
         v,
         w,
@@ -597,10 +583,17 @@
         height,
         face,
         owner.reshape(1, 2 * rows),
-    )
-    shape = (planes, SUB, steps, span)
-    out = bl.reshape(shape) + q.reshape(shape) * below[:, :, None, :] + fb.reshape(shape) * above[:, :, None, :]
-    return out.reshape(u.shape)
+    ]
+    return pl.pallas_call(
+        functools.partial(kernel, gz, gy, nx),
+        out_shape=jax.ShapeDtypeStruct(u.shape, F32),
+        in_specs=[pl.BlockSpec(memory_space=pl.ANY)] * 13,
+        out_specs=pl.BlockSpec(memory_space=pltpu.VMEM),
+        scratch_shapes=scratch,
+        compiler_params=pltpu.CompilerParams(
+            collective_id=0, has_side_effects=True, vmem_limit_bytes=40 * 2**20
+        ),
+    )(*[pltpu.with_memory_space_constraint(x, pltpu.HBM) for x in operands])
 
 
 def solution(mesh):

time: 32.6 us -> 26.5 us (0.81)
  Pallas kernels: 29.9 us -> 25.7 us
  other arithmetic: 1.83 us -> 0 us
    pallas_call x1, Pallas kernels: 29.9 us -> 25.7 us  [local(): pl.pallas_call(functools.partial(kernel, gz, gy, nx), out_shape=jax.Shape...]
    add x1 -> x0, other arithmetic: 1.83 us -> none  [local(): bl.reshape(shape) + q.reshape(shape) * below[:, :, None, :]]
    unnamed x2 -> x1, local copies, waits for them, and re-layouts: 0.69 us -> 0.68 us
where the time goes in v2:
time: 26.5 us; the launch traced here: 26.4 us
  Pallas kernels  25.7 us (97%)
  local copies, waits for them, and re-layouts  0.68 us (3%)
    pallas_call x1, Pallas kernels, local(): pl.pallas_call(functools.partial(kernel, gz, gy, nx), out_shape=jax.Shape...  25.7 us
    unnamed x1, local copies, waits for them, and re-layouts  0.68 us

profile of v2, /device:TPU:1, one launch (start us, length us, event | category | flops | bytes accessed | tf_op | source)
XLA Modules:
  0.0 26.4 jit_solution(18308091141553485040)
XLA Ops:
  0.0 25.7 %shard_map.127 = f32[2,192,128]{2,1,0:T(8,128)S(1)} custom-call(f32[2,192,128]{2,1,0:T(8,128)} %u_hbm.1, f32[2,192,128]{2,1,0:T(8,128)} %v_hbm.1, f32[2,192,128]{2,1,0:T(8,128)} %w_hbm.1, f32[2,192,128]{2,1,0:T(8,128)} %s_hbm.1, f32[3,128]{1,0:T(4,128)} %w_in_hbm.1, f32[1,128]{1,0:T(1,128)} %bitcast.5, f32[128,128]{1,0:T(8,128)} %w_mid_hbm.1, ...), custom_call_target="tpu_custom_call" | custom-call | tf_op jit(solution)/shard_map/pallas_call | solution.py:587
  25.7 0.7 %copy.15 = f32[2,192,128]{2,1,0:T(8,128)} copy(f32[2,192,128]{2,1,0:T(8,128)S(1)} %shard_map.127) | data formatting | bytes 393216

commit v3 on v2

--- a/solution.py
+++ b/solution.py
@@ -165,6 +165,9 @@
     recv_a,
     send_b,
     recv_b,
+    send_d,
+    recv_d,
+    high_ref,
     send_s,
     recv_s,
     load_sem,
@@ -174,6 +177,8 @@
     a_recv,
     b_send,
     b_recv,
+    d_send,
+    d_recv,
     s_send,
     s_recv,
 ):
@@ -181,15 +186,16 @@
     steps = levels // SUB
     total_steps = planes * steps
     nyc = gz // nx
-    roles = (0, 1, gy - 2, gy - 1)
     me = lax.axis_index("gz")
     level = lax.axis_index("gy")
     xx = me // nyc
     yc = me % nyc
-    is_top = level >= gy // 2
-    is_tot = (level == 0) | (level == gy - 1)
-    is_role = is_tot | (level == 1) | (level == gy - 2)
-    role = jnp.where(is_top, level - (gy - 4), level)
+    is_low, is_high = level == 0, level == gy - 1
+    is_top = (level == 1) | is_high
+    is_tot = is_low | is_high
+    is_role = (level <= 2) | is_high
+    role = jnp.where(is_high, 3, level)
+    roles = (0, 1, 2, gy - 1)
 
     start = pl.multiple_of(jnp.where(is_top, levels - WIN, 0), 8)
     load_u = pltpu.make_async_copy(u_hbm, u_ref, load_sem.at[0])
@@ -243,8 +249,20 @@
 
     @pl.loop(1, nx)
     def _(d):
-        for r in roles:
-            greet(lax.rem(xx + d, nx) * nyc + yc, r)
+        for y in roles[:-1]:
+            greet(lax.rem(xx + d, nx) * nyc + yc, y)
+
+    @pl.when(is_low)
+    def _():
+        @pl.loop(1, gz)
+        def _(d):
+            greet(lax.rem(me + d, gz), gy - 1)
+
+    @pl.when(jnp.logical_not(is_low))
+    def _():
+        @pl.loop(1, nx)
+        def _(d):
+            greet(lax.rem(xx + d, nx) * nyc + yc, gy - 1)
 
     @pl.when(is_role)
     def _():
@@ -265,11 +283,31 @@
         packed = step_loop(steps, 8, pack, packed)
     pack_ref[...] = packed
 
+    @pl.when(is_tot)
+    def _():
+        for copy in weights:
+            copy.wait()
+        network(is_top, u_ref, win_ref, w_in_ref, vec_ref, w_mid_ref, cols_ref, wl_ref, samp_ref, table_ref)
+
+    @pl.when(is_role & jnp.logical_not(is_tot))
+    def _():
+        table_ref[...] = jnp.ones_like(table_ref)
+
+    @pl.when(is_role)
+    def _():
+        for copy in lists:
+            copy.wait()
+        binning(is_top, nx, nyc, cell_ref, height_ref, face_ref, owner_ref, table_ref, acc_ref)
+
     base = gy - 1 + 2
 
-    @pl.when(is_role)
+    @pl.when(is_role & jnp.logical_not(is_high))
     def _():
         pl.semaphore_wait(barrier, base + nyc - 1 + (nx - 1) * gy)
+
+    @pl.when(is_high)
+    def _():
+        pl.semaphore_wait(barrier, base + nyc - 1 + (nx - 1) * (gy - 1) + gz - 1)
 
     @pl.when(jnp.logical_not(is_role))
     def _():
@@ -309,6 +347,16 @@
             device_id_type=MESH,
         )
 
+    def copy_d(x, z):
+        return pltpu.make_async_remote_copy(
+            src_ref=send_d.at[z * nx + x],
+            dst_ref=recv_d.at[me],
+            send_sem=d_send,
+            recv_sem=d_recv,
+            device_id=(x * nyc + z, 0),
+            device_id_type=MESH,
+        )
+
     def copy_s(y):
         return pltpu.make_async_remote_copy(
             src_ref=send_s,
@@ -319,27 +367,25 @@
             device_id_type=MESH,
         )
 
-    @pl.when(is_tot)
-    def _():
-        for copy in weights:
-            copy.wait()
-        network(is_top, u_ref, win_ref, w_in_ref, vec_ref, w_mid_ref, cols_ref, wl_ref, samp_ref, table_ref)
-
-    @pl.when(is_role & jnp.logical_not(is_tot))
-    def _():
-        table_ref[...] = jnp.ones_like(table_ref)
-
     @pl.when(is_role)
     def _():
-        for copy in lists:
-            copy.wait()
-        binning(is_top, nx, nyc, cell_ref, height_ref, face_ref, owner_ref, table_ref, acc_ref)
         binned = acc_ref[:, :LANES] + acc_ref[:, LANES:]
+
         send_a[...] = binned.reshape(send_a.shape)
         recv_a[yc] = send_a[yc]
-
         for d in sorted(range(1, nyc), key=lambda d: -min(d, nyc - d)):
             copy_a(lax.rem(yc + d, nyc), yc).start()
+
+    @pl.when(is_high)
+    def _():
+        send_d[...] = (acc_ref[:, :LANES] + acc_ref[:, LANES:]).reshape(send_d.shape)
+        for dx in sorted(range(nx), key=lambda d: -min(d, nx - d)):
+
+            @pl.loop(0, nyc)
+            def _(t, dx=dx):
+                away = (t + 1) // 2
+                dz = jnp.where(t % 2 == 1, nyc // 2 + away, nyc // 2 - away + nyc)
+                copy_d(lax.rem(xx + dx, nx), lax.rem(yc + dz, nyc)).start()
 
     load_s.wait()
     for copy in halo_copies:
@@ -448,14 +494,20 @@
         for x in range(nx):
             send_b[x] = part[2 * x : 2 * x + 2, :]
         recv_b[role * nx + xx] = send_b[xx]
-
         for y in range(gy):
-            for d in sorted(range(1, nx), key=lambda d: -min(d, nx - d)):
-                copy_b(lax.rem(xx + d, nx), y).start()
-
-            @pl.when(level != y)
-            def _(y=y):
-                copy_b(xx, y).start()
+
+            def send_level(y=y):
+                for d in sorted(range(1, nx), key=lambda d: -min(d, nx - d)):
+                    copy_b(lax.rem(xx + d, nx), y).start()
+
+                @pl.when(level != y)
+                def _(y=y):
+                    copy_b(xx, y).start()
+
+            if y:
+                send_level()
+            else:
+                pl.when(jnp.logical_not(is_high))(send_level)
 
     pltpu.make_async_copy(recv_s.at[pl.ds(0, gy - 1)], recv_s.at[pl.ds(0, gy - 1)], s_recv).wait()
 
@@ -483,24 +535,36 @@
             dlt = block(g, 0) * dlt + block(g, 2) + block(g, 3) * betas[g]
             eps = block(g, 0) * eps
 
-    count = 4 * nx
-
-    @pl.when(is_role)
-    def _():
-        pltpu.make_async_copy(recv_b.at[pl.ds(0, count - 1)], recv_b.at[pl.ds(0, count - 1)], b_recv).wait()
-
-    @pl.when(jnp.logical_not(is_role))
-    def _():
-        pltpu.make_async_copy(recv_b, recv_b, b_recv).wait()
-
-    sums = []
-    for r in range(4):
+    def arrive(slots):
+        pltpu.make_async_copy(recv_b.at[pl.ds(0, slots)], recv_b.at[pl.ds(0, slots)], b_recv).wait()
+
+    def gather(r):
         total = recv_b[r * nx]
         for x in range(1, nx):
             total = total + recv_b[r * nx + x]
-        sums.append(total)
-    stress_low = sums[0] / jnp.maximum(sums[1], 1.0)
-    stress_top = sums[3] / jnp.maximum(sums[2], 1.0)
+        return total
+
+    @pl.when(is_low)
+    def _():
+        arrive(3 * nx - 1)
+        pltpu.make_async_copy(recv_d, recv_d, d_recv).wait()
+        parts = [recv_d[i] for i in range(4)]
+        for i in range(4, gz):
+            parts[i % 4] = parts[i % 4] + recv_d[i]
+        high_ref[...] = (parts[0] + parts[1]) + (parts[2] + parts[3])
+
+    @pl.when(is_role & jnp.logical_not(is_low))
+    def _():
+        arrive(4 * nx - 1)
+        high_ref[...] = gather(3)
+
+    @pl.when(jnp.logical_not(is_role))
+    def _():
+        arrive(4 * nx)
+        high_ref[...] = gather(3)
+
+    stress_low = gather(0) / jnp.maximum(gather(2), 1.0)
+    stress_top = high_ref[...] / jnp.maximum(gather(1), 1.0)
     f_in = alpha * stress_low + beta
     b_in = gamma * stress_low + delta + epsilon * stress_top
     for p in range(planes):
@@ -520,10 +584,19 @@
 
     @pl.when(is_role)
     def _():
-        pltpu.make_async_copy(send_a.at[pl.ds(0, nyc - 1)], send_a.at[pl.ds(0, nyc - 1)], a_send).wait()
-        for _ in range(gy - 1):
+        left_a, left_b = send_a.at[pl.ds(0, nyc - 1)], send_b.at[pl.ds(0, nx - 1)]
+        pltpu.make_async_copy(left_a, left_a, a_send).wait()
+        pltpu.make_async_copy(left_b, left_b, b_send).wait()
+        for _ in range(gy - 2):
             pltpu.make_async_copy(send_b, send_b, b_send).wait()
-        pltpu.make_async_copy(send_b.at[pl.ds(0, nx - 1)], send_b.at[pl.ds(0, nx - 1)], b_send).wait()
+
+    @pl.when(is_role & jnp.logical_not(is_high))
+    def _():
+        pltpu.make_async_copy(send_b, send_b, b_send).wait()
+
+    @pl.when(is_high)
+    def _():
+        pltpu.make_async_copy(send_d, send_d, d_send).wait()
 
 
 def local(gz, gy, nx, *args):
@@ -563,12 +636,15 @@
         vmem((nyc, 2 * nx, span), F32),
         vmem((nx, 2, span), F32),
         vmem((4 * nx, 2, span), F32),
+        vmem((gz, 2, span), F32),
+        vmem((gz, 2, span), F32),
+        vmem((2, span), F32),
         vmem((8, span), F32),
         vmem((gy, 8, span), F32),
         pltpu.SemaphoreType.DMA((13,)),
         pltpu.SemaphoreType.DMA((2,)),
         pltpu.SemaphoreType.DMA((2,)),
-    ] + [pltpu.SemaphoreType.DMA] * 6
+    ] + [pltpu.SemaphoreType.DMA] * 8
     operands = [
         u,
         v,

time: 26.5 us -> 25.9 us (0.977)
  Pallas kernels: 25.7 us -> 25.1 us
    pallas_call x1, Pallas kernels: 25.7 us -> 25.1 us  [local(): pl.pallas_call(functools.partial(kernel, gz, gy, nx), out_shape=jax.Shape...]
where the time goes in v3:
time: 25.9 us; the launch traced here: 25.8 us
  Pallas kernels  25.1 us (97%)
  local copies, waits for them, and re-layouts  0.68 us (3%)
    pallas_call x1, Pallas kernels, local(): pl.pallas_call(functools.partial(kernel, gz, gy, nx), out_shape=jax.Shape...  25.1 us
    unnamed x1, local copies, waits for them, and re-layouts  0.68 us

profile of v3, /device:TPU:1, one launch (start us, length us, event | category | flops | bytes accessed | tf_op | source)
XLA Modules:
  0.0 25.8 jit_solution(18354410063895410119)
XLA Ops:
  0.0 25.1 %shard_map.127 = f32[2,192,128]{2,1,0:T(8,128)S(1)} custom-call(f32[2,192,128]{2,1,0:T(8,128)} %u_hbm.1, f32[2,192,128]{2,1,0:T(8,128)} %v_hbm.1, f32[2,192,128]{2,1,0:T(8,128)} %w_hbm.1, f32[2,192,128]{2,1,0:T(8,128)} %s_hbm.1, f32[3,128]{1,0:T(4,128)} %w_in_hbm.1, f32[1,128]{1,0:T(1,128)} %bitcast.5, f32[128,128]{1,0:T(8,128)} %w_mid_hbm.1, ...), custom_call_target="tpu_custom_call" | custom-call | tf_op jit(solution)/shard_map/pallas_call | solution.py:663
  25.1 0.7 %copy.15 = f32[2,192,128]{2,1,0:T(8,128)} copy(f32[2,192,128]{2,1,0:T(8,128)S(1)} %shard_map.127) | data formatting | bytes 393216

commit v4 on v3

--- a/solution.py
+++ b/solution.py
@@ -77,10 +77,10 @@
     rows = cell_ref.shape[1]
     planes = table_ref.shape[0] // HMAX
     acc_ref[...] = jnp.zeros_like(acc_ref)
-    bins = acc_ref.shape[0]
+    bins = acc_ref.shape[0] // 2
     row = lax.broadcasted_iota(jnp.int32, (SUB, LANES), 0)
-    rows_iota = lax.broadcasted_iota(jnp.int32, (LANES, KB), 0)
-    bins_iota = lax.broadcasted_iota(jnp.int32, (bins, KB), 0)
+    rows_iota = lax.broadcasted_iota(jnp.int32, (LANES, KB), 0).astype(F32).astype(BF16)
+    bins_iota = lax.broadcasted_iota(jnp.int32, (bins, KB), 0).astype(F32).astype(BF16)
 
     @pl.loop(0, rows // KB)
     def _(i):
@@ -108,13 +108,13 @@
         rest = value - first
         low = face % LANES
         high = (owner % nyc) * (2 * nx) + (owner // nyc) * 2 + face // LANES
-        onto = jnp.where(bins_iota == high, 1.0, 0.0).astype(BF16)
-        named = rows_iota == low
+        named = bins_iota == high.astype(F32).astype(BF16)
         carried = jnp.concatenate(
-            [jnp.where(named, first, 0.0).astype(BF16), jnp.where(named, rest, 0.0).astype(BF16)], axis=0
-        )
+            [jnp.where(named, first.astype(BF16), BF16(0.0)), jnp.where(named, rest.astype(BF16), BF16(0.0))], axis=0
+        )
+        onto = jnp.where(rows_iota == low.astype(F32).astype(BF16), BF16(1.0), BF16(0.0))
         acc_ref[...] += lax.dot_general(
-            onto, carried, (((1,), (1,)), ((), ())), preferred_element_type=F32
+            carried, onto, (((1,), (1,)), ((), ())), preferred_element_type=F32
         )
 
 
@@ -181,6 +181,7 @@
     d_recv,
     s_send,
     s_recv,
+    ready,
 ):
     planes, levels, _ = u_ref.shape
     steps = levels // SUB
@@ -193,7 +194,8 @@
     is_low, is_high = level == 0, level == gy - 1
     is_top = (level == 1) | is_high
     is_tot = is_low | is_high
-    is_role = (level <= 2) | is_high
+    is_early, is_direct = level <= 2, level <= 1
+    is_role = is_early | is_high
     role = jnp.where(is_high, 3, level)
     roles = (0, 1, 2, gy - 1)
 
@@ -243,32 +245,44 @@
     greet(left, level)
     greet(right, level)
 
-    @pl.loop(1, gy)
-    def _(d):
-        greet(me, lax.rem(level + d, gy))
-
-    @pl.loop(1, nx)
-    def _(d):
-        for y in roles[:-1]:
-            greet(lax.rem(xx + d, nx) * nyc + yc, y)
-
-    @pl.when(is_low)
+    @pl.when(is_early)
+    def _():
+        @pl.loop(1, nx)
+        def _(d):
+            for y in range(3):
+                greet(lax.rem(xx + d, nx) * nyc + yc, y)
+
+    @pl.when(is_role)
+    def _():
+        @pl.loop(1, nyc)
+        def _(d):
+            greet(xx * nyc + lax.rem(yc + d, nyc), level)
+
+    for y in range(gy):
+        meets = (level != y) if y >= 3 else is_early & (level != y)
+
+        @pl.when(meets)
+        def _(y=y):
+            greet(me, y)
+
+    @pl.when(is_early)
+    def _():
+        @pl.loop(1, nx)
+        def _(d):
+            for y in range(3, gy - 1):
+                greet(lax.rem(xx + d, nx) * nyc + yc, y)
+
+    @pl.when(jnp.logical_not(is_direct))
+    def _():
+        @pl.loop(1, nx)
+        def _(d):
+            greet(lax.rem(xx + d, nx) * nyc + yc, gy - 1)
+
+    @pl.when(is_direct)
     def _():
         @pl.loop(1, gz)
         def _(d):
             greet(lax.rem(me + d, gz), gy - 1)
-
-    @pl.when(jnp.logical_not(is_low))
-    def _():
-        @pl.loop(1, nx)
-        def _(d):
-            greet(lax.rem(xx + d, nx) * nyc + yc, gy - 1)
-
-    @pl.when(is_role)
-    def _():
-        @pl.loop(1, nyc)
-        def _(d):
-            greet(xx * nyc + lax.rem(yc + d, nyc), level)
 
     lane = lax.broadcasted_iota(jnp.int32, (SUB, LANES), 1)
     row = lax.broadcasted_iota(jnp.int32, (SUB, LANES), 0)
@@ -301,17 +315,25 @@
 
     base = gy - 1 + 2
 
-    @pl.when(is_role & jnp.logical_not(is_high))
-    def _():
-        pl.semaphore_wait(barrier, base + nyc - 1 + (nx - 1) * gy)
+    @pl.when(is_early)
+    def _():
+        pl.semaphore_wait(barrier, 4 + nyc - 1 + (nx - 1) * 3)
 
     @pl.when(is_high)
     def _():
-        pl.semaphore_wait(barrier, base + nyc - 1 + (nx - 1) * (gy - 1) + gz - 1)
+        pl.semaphore_wait(barrier, base + nyc - 1 + (nx - 1) * (gy - 2) + 2 * (gz - 1))
 
     @pl.when(jnp.logical_not(is_role))
     def _():
-        pl.semaphore_wait(barrier, base)
+        pl.semaphore_wait(barrier, base + (nx - 1) * 3)
+
+    @pl.when(jnp.logical_not(is_early))
+    def _():
+        for y in range(3):
+            for d in range(nx):
+                pl.semaphore_signal(
+                    ready, inc=1, device_id=(lax.rem(xx + d, nx) * nyc + yc, y), device_id_type=MESH
+                )
 
     halo_copies = [
         pltpu.make_async_remote_copy(
@@ -347,13 +369,13 @@
             device_id_type=MESH,
         )
 
-    def copy_d(x, z):
+    def copy_d(x, z, y):
         return pltpu.make_async_remote_copy(
             src_ref=send_d.at[z * nx + x],
             dst_ref=recv_d.at[me],
             send_sem=d_send,
             recv_sem=d_recv,
-            device_id=(x * nyc + z, 0),
+            device_id=(x * nyc + z, y),
             device_id_type=MESH,
         )
 
@@ -369,23 +391,36 @@
 
     @pl.when(is_role)
     def _():
-        binned = acc_ref[:, :LANES] + acc_ref[:, LANES:]
+        binned = acc_ref[: 2 * gz, :] + acc_ref[2 * gz :, :]
 
         send_a[...] = binned.reshape(send_a.shape)
         recv_a[yc] = send_a[yc]
+
+    ny = nyc // 2
+    early = list(range(-(-ny // 2))) + list(range(ny - 1, -(-ny // 2) - 1, -1))
+
+    @pl.when(is_high)
+    def _():
+        send_d[...] = (acc_ref[: 2 * gz, :] + acc_ref[2 * gz :, :]).reshape(send_d.shape)
+        for x in range(nx):
+            for c in (1, 0):
+                copy_d(x, 2 * early[0] + c, 0).start()
+
+    @pl.when(is_role)
+    def _():
         for d in sorted(range(1, nyc), key=lambda d: -min(d, nyc - d)):
             copy_a(lax.rem(yc + d, nyc), yc).start()
 
     @pl.when(is_high)
     def _():
-        send_d[...] = (acc_ref[:, :LANES] + acc_ref[:, LANES:]).reshape(send_d.shape)
-        for dx in sorted(range(nx), key=lambda d: -min(d, nx - d)):
-
-            @pl.loop(0, nyc)
-            def _(t, dx=dx):
-                away = (t + 1) // 2
-                dz = jnp.where(t % 2 == 1, nyc // 2 + away, nyc // 2 - away + nyc)
-                copy_d(lax.rem(xx + dx, nx), lax.rem(yc + dz, nyc)).start()
+        for x in range(nx):
+            for c in (1, 0):
+                copy_d(x, 2 * early[0] + c, 1).start()
+        for y in early[1:]:
+            for level_to in range(2):
+                for x in range(nx):
+                    for c in (1, 0):
+                        copy_d(x, 2 * y + c, level_to).start()
 
     load_s.wait()
     for copy in halo_copies:
@@ -434,9 +469,10 @@
             value = keep * value + gain * lf_ref[p, b]
             response = keep * response + gain * ff_ref[p, b]
             factor = keep * factor
-            bl_ref[p, b] = value
-            q_ref[p, b] = response
-            fb_ref[p, b] = factor
+            at = pl.ds(b, SUB, stride=steps)
+            bl_ref[p, at, :] = value
+            q_ref[p, at, :] = response
+            fb_ref[p, at, :] = factor
             out += [value, response, factor]
         return tuple(out)
 
@@ -481,9 +517,27 @@
     send_s[...] = summary
     recv_s[level] = summary
 
-    @pl.loop(1, gy)
-    def _(d):
-        copy_s(lax.rem(level + d, gy)).start()
+    def summary_to(levels_to):
+        for y in levels_to:
+
+            @pl.when(level != y)
+            def _(y=y):
+                copy_s(y).start()
+
+    def second_to(levels_to):
+        for y in levels_to:
+            for d in sorted(range(1, nx), key=lambda d: -min(d, nx - d)):
+                copy_b(lax.rem(xx + d, nx), y).start()
+
+            @pl.when(level != y)
+            def _(y=y):
+                copy_b(xx, y).start()
+
+    summary_to(range(3))
+
+    @pl.when(jnp.logical_not(is_early))
+    def _():
+        summary_to(range(3, gy))
 
     @pl.when(is_role)
     def _():
@@ -494,20 +548,17 @@
         for x in range(nx):
             send_b[x] = part[2 * x : 2 * x + 2, :]
         recv_b[role * nx + xx] = send_b[xx]
-        for y in range(gy):
-
-            def send_level(y=y):
-                for d in sorted(range(1, nx), key=lambda d: -min(d, nx - d)):
-                    copy_b(lax.rem(xx + d, nx), y).start()
-
-                @pl.when(level != y)
-                def _(y=y):
-                    copy_b(xx, y).start()
-
-            if y:
-                send_level()
-            else:
-                pl.when(jnp.logical_not(is_high))(send_level)
+
+    @pl.when(is_early)
+    def _():
+        second_to(range(3))
+        pl.semaphore_wait(ready, nx * (gy - 3))
+        summary_to(range(3, gy))
+        second_to(range(3, gy))
+
+    @pl.when(is_high)
+    def _():
+        second_to(range(2, gy))
 
     pltpu.make_async_copy(recv_s.at[pl.ds(0, gy - 1)], recv_s.at[pl.ds(0, gy - 1)], s_recv).wait()
 
@@ -544,7 +595,7 @@
             total = total + recv_b[r * nx + x]
         return total
 
-    @pl.when(is_low)
+    @pl.when(is_direct)
     def _():
         arrive(3 * nx - 1)
         pltpu.make_async_copy(recv_d, recv_d, d_recv).wait()
@@ -553,7 +604,7 @@
             parts[i % 4] = parts[i % 4] + recv_d[i]
         high_ref[...] = (parts[0] + parts[1]) + (parts[2] + parts[3])
 
-    @pl.when(is_role & jnp.logical_not(is_low))
+    @pl.when(is_role & jnp.logical_not(is_direct))
     def _():
         arrive(4 * nx - 1)
         high_ref[...] = gather(3)
@@ -572,11 +623,11 @@
         below = pf * f_in[p : p + 1] + lf
         above = pb * b_in[p : p + 1] + cb + qb * f_in[p : p + 1]
 
-        def finish(b, _, p=p, below=below, above=above):
-            out_ref[p, pl.ds(b, SUB, stride=steps), :] = bl_ref[p, b] + q_ref[p, b] * below + fb_ref[p, b] * above
-            return _
-
-        step_loop(steps, steps, finish, 0)
+        for j in range(SUB):
+            cut = slice(j * steps, (j + 1) * steps)
+            out_ref[p, cut, :] = (
+                bl_ref[p, cut, :] + q_ref[p, cut, :] * below[j : j + 1] + fb_ref[p, cut, :] * above[j : j + 1]
+            )
 
     for copy in halo_copies:
         copy.wait_send()
@@ -587,16 +638,18 @@
         left_a, left_b = send_a.at[pl.ds(0, nyc - 1)], send_b.at[pl.ds(0, nx - 1)]
         pltpu.make_async_copy(left_a, left_a, a_send).wait()
         pltpu.make_async_copy(left_b, left_b, b_send).wait()
-        for _ in range(gy - 2):
+        for _ in range(gy - 3):
             pltpu.make_async_copy(send_b, send_b, b_send).wait()
 
-    @pl.when(is_role & jnp.logical_not(is_high))
-    def _():
-        pltpu.make_async_copy(send_b, send_b, b_send).wait()
+    @pl.when(is_early)
+    def _():
+        for _ in range(2):
+            pltpu.make_async_copy(send_b, send_b, b_send).wait()
 
     @pl.when(is_high)
     def _():
-        pltpu.make_async_copy(send_d, send_d, d_send).wait()
+        for _ in range(2):
+            pltpu.make_async_copy(send_d, send_d, d_send).wait()
 
 
 def local(gz, gy, nx, *args):
@@ -621,15 +674,15 @@
         vmem((2 * span, 2 * span), BF16),
         vmem((3, planes * HMAX, span), F32),
         vmem((planes * HMAX, span), F32),
-        vmem((2 * gz, 2 * span), F32),
+        vmem((4 * gz, span), F32),
         vmem((planes, steps, SUB, span), F32),
         vmem((planes, steps, SUB, span), F32),
         vmem((planes, steps, SUB, span), F32),
         vmem((planes, steps, SUB, span), F32),
         vmem((planes, steps, SUB, span), F32),
-        vmem((planes, steps, SUB, span), F32),
-        vmem((planes, steps, SUB, span), F32),
-        vmem((planes, steps, SUB, span), F32),
+        vmem(u.shape, F32),
+        vmem(u.shape, F32),
+        vmem(u.shape, F32),
         vmem((SUB, span), F32),
         vmem((2, SUB, span), F32),
         vmem((nyc, 2 * nx, span), F32),
@@ -644,7 +697,7 @@
         pltpu.SemaphoreType.DMA((13,)),
         pltpu.SemaphoreType.DMA((2,)),
         pltpu.SemaphoreType.DMA((2,)),
-    ] + [pltpu.SemaphoreType.DMA] * 8
+    ] + [pltpu.SemaphoreType.DMA] * 8 + [pltpu.SemaphoreType.REGULAR]
     operands = [
         u,
         v,

time: 25.9 us -> 24.6 us (0.950)
  Pallas kernels: 25.1 us -> 23.7 us
    pallas_call x1, Pallas kernels: 25.1 us -> 23.7 us  [local(): pl.pallas_call(functools.partial(kernel, gz, gy, nx), out_shape=jax.Shape...]
where the time goes in v4:
time: 24.6 us; the launch traced here: 24.4 us
  Pallas kernels  23.7 us (96%)
  local copies, waits for them, and re-layouts  0.68 us (3%)
    pallas_call x1, Pallas kernels, local(): pl.pallas_call(functools.partial(kernel, gz, gy, nx), out_shape=jax.Shape...  23.7 us
    unnamed x1, local copies, waits for them, and re-layouts  0.68 us

profile of v4, /device:TPU:1, one launch (start us, length us, event | category | flops | bytes accessed | tf_op | source)
XLA Modules:
  0.0 24.4 jit_solution(16430952610442493070)
XLA Ops:
  0.0 23.7 %shard_map.127 = f32[2,192,128]{2,1,0:T(8,128)S(1)} custom-call(f32[2,192,128]{2,1,0:T(8,128)} %u_hbm.1, f32[2,192,128]{2,1,0:T(8,128)} %v_hbm.1, f32[2,192,128]{2,1,0:T(8,128)} %w_hbm.1, f32[2,192,128]{2,1,0:T(8,128)} %s_hbm.1, f32[3,128]{1,0:T(4,128)} %w_in_hbm.1, f32[1,128]{1,0:T(1,128)} %bitcast.5, f32[128,128]{1,0:T(8,128)} %w_mid_hbm.1, ...), custom_call_target="tpu_custom_call" | custom-call | tf_op jit(solution)/shard_map/pallas_call | solution.py:716
  23.8 0.7 %copy.15 = f32[2,192,128]{2,1,0:T(8,128)} copy(f32[2,192,128]{2,1,0:T(8,128)S(1)} %shard_map.127) | data formatting | bytes 393216

commit v5 on v4

--- a/solution.py
+++ b/solution.py
@@ -389,13 +389,6 @@
             device_id_type=MESH,
         )
 
-    @pl.when(is_role)
-    def _():
-        binned = acc_ref[: 2 * gz, :] + acc_ref[2 * gz :, :]
-
-        send_a[...] = binned.reshape(send_a.shape)
-        recv_a[yc] = send_a[yc]
-
     ny = nyc // 2
     early = list(range(-(-ny // 2))) + list(range(ny - 1, -(-ny // 2) - 1, -1))
 
@@ -405,6 +398,13 @@
         for x in range(nx):
             for c in (1, 0):
                 copy_d(x, 2 * early[0] + c, 0).start()
+
+    @pl.when(is_role)
+    def _():
+        binned = acc_ref[: 2 * gz, :] + acc_ref[2 * gz :, :]
+
+        send_a[...] = binned.reshape(send_a.shape)
+        recv_a[yc] = send_a[yc]
 
     @pl.when(is_role)
     def _():

time: 24.6 us -> 24.6 us (level)
  no operation moved by 1% of the time
where the time goes in v5:
time: 24.6 us; the launch traced here: 24.4 us
  Pallas kernels  23.7 us (96%)
  local copies, waits for them, and re-layouts  0.68 us (3%)
    pallas_call x1, Pallas kernels, local(): pl.pallas_call(functools.partial(kernel, gz, gy, nx), out_shape=jax.Shape...  23.7 us
    unnamed x1, local copies, waits for them, and re-layouts  0.68 us

profile of v5, /device:TPU:1, one launch (start us, length us, event | category | flops | bytes accessed | tf_op | source)
XLA Modules:
  0.0 24.4 jit_solution(4575014003874969857)
XLA Ops:
  0.0 23.7 %shard_map.127 = f32[2,192,128]{2,1,0:T(8,128)S(1)} custom-call(f32[2,192,128]{2,1,0:T(8,128)} %u_hbm.1, f32[2,192,128]{2,1,0:T(8,128)} %v_hbm.1, f32[2,192,128]{2,1,0:T(8,128)} %w_hbm.1, f32[2,192,128]{2,1,0:T(8,128)} %s_hbm.1, f32[3,128]{1,0:T(4,128)} %w_in_hbm.1, f32[1,128]{1,0:T(1,128)} %bitcast.5, f32[128,128]{1,0:T(8,128)} %w_mid_hbm.1, ...), custom_call_target="tpu_custom_call" | custom-call | tf_op jit(solution)/shard_map/pallas_call | solution.py:716
  23.8 0.7 %copy.15 = f32[2,192,128]{2,1,0:T(8,128)} copy(f32[2,192,128]{2,1,0:T(8,128)S(1)} %shard_map.127) | data formatting | bytes 393216
